TPU v7x, 32 devices: a whole 2x2x4 slice. The times are simulated.
32 devices in a mesh: shard: 8 (over z, y), ctx: 2 (over x), tp: 2 (over core).
Axes of the slice: x: 2, y: 2, z: 4, core: 2. Of those that a mesh axis runs over, the one named last changes fastest.
Arguments:
- inputs: bfloat16 [2, 8192, 1024], P(None, ('shard', 'ctx')), may hold values from -6 to 6
- cotangent: bfloat16 [2, 8192, 1024], P(None, ('shard', 'ctx')), may hold values from -6 to 6
- lengths: int32 [2, 8], P(None, 'shard'), may hold values from 256 to 1024, as said below
- buckets: int32 [1024, 1024], P('ctx'), may hold values from 0 to 31, as said below
- query_weight: bfloat16 [1024, 1024], P(('shard', 'ctx'), 'tp'), may hold values from -0.09375 to 0.09375
- key_weight: bfloat16 [1024, 1024], P(('shard', 'ctx'), 'tp'), may hold values from -0.09375 to 0.09375
- value_weight: bfloat16 [1024, 1024], P(('shard', 'ctx'), 'tp'), may hold values from -0.1875 to 0.1875
- projection_weight: bfloat16 [1024, 1024], P(('shard', 'ctx'), 'tp'), may hold values from -1 to 1
- gate_weight: bfloat16 [1024, 2816], P(('shard', 'ctx'), 'tp'), may hold values from -0.1875 to 0.1875
- up_weight: bfloat16 [1024, 2816], P(('shard', 'ctx'), 'tp'), may hold values from -0.1875 to 0.1875
- down_weight: bfloat16 [1024, 2816], P(('shard', 'ctx'), 'tp'), may hold values from -0.21875 to 0.21875
- attention_gain: bfloat16 [1024], P(('shard', 'ctx')), may hold values from 0.099609375 to 1.8984375
- feedforward_gain: bfloat16 [1024], P(('shard', 'ctx')), may hold values from 0.099609375 to 1.8984375
- bias_table: bfloat16 [32, 16], P(None, 'tp'), may hold values from -4 to 4
Outputs:
- output: bfloat16 [2, 8192, 1024], P(None, ('shard', 'ctx'))
- input_grad: float32 [2, 8192, 1024], P(None, ('shard', 'ctx'))
- query_grad: float32 [1024, 1024], P(('shard', 'ctx'), 'tp')
- key_grad: float32 [1024, 1024], P(('shard', 'ctx'), 'tp')
- value_grad: float32 [1024, 1024], P(('shard', 'ctx'), 'tp')
- projection_grad: float32 [1024, 1024], P(('shard', 'ctx'), 'tp')
- gate_grad: float32 [1024, 2816], P(('shard', 'ctx'), 'tp')
- up_grad: float32 [1024, 2816], P(('shard', 'ctx'), 'tp')
- down_grad: float32 [1024, 2816], P(('shard', 'ctx'), 'tp')
- attention_gain_grad: float32 [1024], P(('shard', 'ctx'))
- feedforward_gain_grad: float32 [1024], P(('shard', 'ctx'))
- table_grad: float32 [32, 16], P(None, 'tp')
Inputs may be any that keep to these rules, and one draw needn't show every extreme that they name: For every sequence index s, at least one of the 2 micro-batches has lengths[m, s] = 1024. T5's bidirectional bucket (16 buckets each way, exact below a distance of 8, logarithmic up to 128) of key position minus query position, where the position ids rise by 1 or 2 from slot to slot.
All inputs are finite; a program needn't handle non-finite values.
Results may differ from a plain program's by a relative error of at most 0.017.
The roundings to bfloat16 on the way count: a program that leaves them out, or rounds other values in their place, can miss the bound.
Values may be sent and summed in bfloat16 or wider, within the bound.
A program may use at most 256 MiB of HBM per device.

v0:
```python
import functools

import jax
import jax.numpy as jnp
from jax import lax
from jax.experimental import pallas as pl
from jax.experimental.pallas import tpu as pltpu
from jax.sharding import PartitionSpec as P

EPSILON = 1e-06
GELU_ROOT = 0.7978845608028654
GELU_CUBIC = 0.044715
MESH = pl.DeviceIdType.MESH
MIB = 1024 * 1024


BAND = 3
BLOCK = 128


def lane_head(rows, width, which):
    lanes = lax.broadcasted_iota(jnp.int32, (rows, width), 1)
    half = width // 2
    return (lanes < half) if which == 0 else (lanes >= half)


def band_start(row_block, blocks):
    return jnp.clip(row_block - 1, 0, blocks - BAND)


def split_columns(start, stop, pieces):
    tiles = (stop - start) // 128
    edges = [start + 128 * (tiles * i // pieces) for i in range(pieces + 1)]
    return [(a, b) for a, b in zip(edges, edges[1:]) if b > a]


class Place:
    def __init__(self, shard_size):
        self.deep = shard_size // 2
        shard = lax.axis_index("shard")
        self.z = shard // 2
        self.y = shard % 2
        self.x = lax.axis_index("ctx")
        self.c = lax.axis_index("tp")

    def device(self, z=None, y=None, x=None, c=None):
        z = self.z if z is None else z
        y = self.y if y is None else y
        x = self.x if x is None else x
        c = self.c if c is None else c
        return (z * 2 + y, x, c)

    def line(self, distance):
        return (self.z + distance) % self.deep

    def peers(self):
        others = [self.device(z=self.line(d)) for d in range(1, self.deep)]
        return others + [self.device(y=1 - self.y), self.device(x=1 - self.x), self.device(c=1 - self.c)]


def meet(place):
    barrier = pltpu.get_barrier_semaphore()
    peers = place.peers()
    for peer in peers:
        pl.semaphore_signal(barrier, inc=1, device_id=peer, device_id_type=MESH)
    pl.semaphore_wait(barrier, len(peers))


def send(source, target, send_sem, recv_sem, device):
    return pltpu.make_async_remote_copy(
        src_ref=source, dst_ref=target, send_sem=send_sem, recv_sem=recv_sem, device_id=device, device_id_type=MESH
    )


LAST = (((1,), (1,)), ((), ()))
FIRST = (((0,), (0,)), ((), ()))
HIDDEN_STEP = 256
HALF_BUCKETS = 16


def hidden_steps(hidden):
    return [min(HIDDEN_STEP, hidden - at) for at in range(0, hidden, HIDDEN_STEP)]


class Gather:
    def __init__(self, place, pieces, own_ref, full_ref, send_sem, recv_sem):
        self.place, self.pieces, self.own, self.full = place, pieces, own_ref, full_ref
        self.send_sem, self.recv_sem = send_sem, recv_sem
        self.queue = []

    def held(self, piece, hop):
        a, b, order = self.pieces[piece]
        place, done = self.place, order[:hop]
        at = [slice(None) if name in done else getattr(place, name) for name in "zyx"]
        return self.full.at[at[0], at[1], at[2], :, a:b]

    def copies(self, piece, hop):
        place = self.place
        a, b, order = self.pieces[piece]
        target = self.held(piece, hop)
        source = self.own.at[:, a:b] if hop == 0 else target
        name = order[hop]
        if name == "z":
            peers = [place.device(z=place.line(d)) for d in range(1, place.deep)]
        elif name == "y":
            peers = [place.device(y=1 - place.y)]
        else:
            peers = [place.device(x=1 - place.x)]
        return [
            send(source, target, self.send_sem.at[piece, hop, i], self.recv_sem.at[piece, hop, i], peer)
            for i, peer in enumerate(peers)
        ]

    def start(self, piece, hop):
        for copy in self.copies(piece, hop):
            copy.start()

    def arrive(self, piece, hop):
        for copy in self.copies(piece, hop):
            copy.wait_recv()

    def sent(self):
        for piece in range(len(self.pieces)):
            for hop in range(3):
                for copy in self.copies(piece, hop):
                    copy.wait_send()

    def plan(self, window):
        count = len(self.pieces)
        self.window = window

        def second(piece):
            def act():
                self.arrive(piece, 0)
                self.start(piece, 1)
                if piece + window < count:
                    self.start(piece + window, 0)
            return act

        def third(piece):
            def act():
                self.arrive(piece, 1)
                self.start(piece, 2)
            return act

        for piece in range(count + 1):
            if piece < count:
                self.queue.append((None, second(piece)))
            if piece > 0:
                self.queue.append((piece - 1, third(piece - 1)))
        for piece in range(min(window, count)):
            self.start(piece, 0)

    def run(self, steps):
        for _ in range(min(steps, len(self.queue))):
            self.queue.pop(0)[1]()

    def take(self, steps):
        taken, self.queue = self.queue[:steps], self.queue[steps:]
        return [act for _, act in taken]

    def need(self, pieces):
        for piece in pieces:
            while any(mark == piece for mark, _ in self.queue):
                self.run(1)
        for piece in pieces:
            self.arrive(piece, 2)


def query_aux(table, step, blocks):
    parts = []
    lanes = lax.broadcasted_iota(jnp.int32, (BLOCK, 128), 1)
    buckets = 2 * HALF_BUCKETS
    below = jnp.broadcast_to(table[0:1, HALF_BUCKETS - 1 : HALF_BUCKETS], (BLOCK, 128))
    above = jnp.broadcast_to(table[0:1, buckets - 1 : buckets], (BLOCK, 128))
    for sub in range(2):
        start = band_start(2 * step + sub, blocks)
        value = jnp.where(lanes < start, below, 0.0)
        value = jnp.where((lanes >= start + BAND) & (lanes < blocks), above, value)
        parts.append(jnp.where(lanes == blocks, 1.0, value))
    return jnp.concatenate(parts, axis=0).astype(jnp.bfloat16)


def gelu_all(gate):
    square = gate * gate
    tangent = jnp.tanh(GELU_ROOT * (gate + GELU_CUBIC * square * gate))
    value = 0.5 * gate * (1.0 + tangent)
    slope = 0.5 * (1.0 + tangent) + 0.5 * gate * (1.0 - tangent * tangent) * (
        GELU_ROOT + (3.0 * GELU_CUBIC * GELU_ROOT) * square
    )
    return value, slope


def front_kernel(
    shard_size, pieces, window, sizes,
    lengths_ref, gains_ref, query_ref, key_ref, value_ref, project_ref, gate_ref, up_ref, down_ref,
    inputs_ref, cots_ref, buckets_ref, table_ref,
    full_ref, normed_out, qkv_out, bandt_out, biast_out, grads_out, attended_out, tokens_own_ref,
    lse_ref, output_ref, middle_grad_ref, gain_ref,
    own_ref, tok, cot, band, bandt, bias, biast, kaux, gain_buf, qkv, normed, scores, attended, project_w,
    normal, away, arrived, two_t, low_t, acc_out, acc_two, w_buf, g_buf, hid, ggate, gup,
    send_sem, recv_sem, near_send, near_recv, local_sem, w_sem, g_sem, own_sem, bt_sem,
):
    inner, hidden = sizes
    length, width = tok.shape
    half, quarter = length // 2, length // 4
    heads, blocks = bias.shape[:2]
    pairs = heads // 2
    deep = shard_size // 2
    low = jnp.bfloat16
    place = Place(shard_size)
    x, c = place.x, place.c
    at_q = 128
    at_project = at_q + 3 * inner
    at_hidden = at_project + inner
    steps = hidden_steps(hidden)
    per_step = 2
    first_hidden_piece = len(pieces) - per_step * len(steps)
    project_pieces = [i for i, (a, b, _) in enumerate(pieces) if at_project <= a < at_hidden]
    qkv_pieces = [i for i, (a, b, _) in enumerate(pieces) if a < at_project]

    def own_load(i, source, target):
        return pltpu.make_async_copy(source, target, local_sem.at[i])

    parts, at = [], 0
    for ref in (gains_ref, query_ref, key_ref, value_ref, project_ref):
        parts.append((ref, at))
        at += ref.shape[1]
    own_loads = [
        pltpu.make_async_copy(ref, own_ref.at[:, at : at + ref.shape[1]], own_sem.at[i]) for i, (ref, at) in enumerate(parts)
    ]
    for j, n in enumerate(steps):
        for k, ref in enumerate((gate_ref, up_ref, down_ref)):
            at = at_hidden + 3 * HIDDEN_STEP * j + k * n
            own_loads.append(
                pltpu.make_async_copy(
                    ref.at[:, HIDDEN_STEP * j : HIDDEN_STEP * j + n], own_ref.at[:, at : at + n], own_sem.at[len(own_loads)]
                )
            )

    def band_source(block):
        start = pl.multiple_of(band_start(block, blocks) * BLOCK, BLOCK)
        first = block - x * (blocks // 2)
        return buckets_ref.at[pl.ds(pl.multiple_of(first * BLOCK, BLOCK), BLOCK), pl.ds(start, BAND * BLOCK)]

    own_tok = own_load(0, inputs_ref.at[x], tok.at[pl.ds(x * half, half)])
    own_cot = own_load(1, cots_ref.at[x], cot.at[pl.ds(x * half, half)])
    own_bands = [
        own_load(13 + i, band_source(x * (blocks // 2) + i), band.at[x * (blocks // 2) + i]) for i in range(blocks // 2)
    ]
    own_full = own_load(3, own_ref, full_ref.at[place.z, place.y, x])
    for copy in (*own_loads, *own_bands, own_tok, own_cot):
        copy.start()
    meet(place)
    for copy in own_loads:
        copy.wait()
    own_full.start()

    gather = Gather(place, pieces, own_ref, full_ref, send_sem, recv_sem)
    to_x, to_c = place.device(x=1 - x), place.device(c=1 - c)

    def x_rows(sender_x, sender_c):
        return pl.ds(sender_x * half + sender_c * quarter, quarter)

    def near(i, source, target, device):
        return send(source, target, near_send.at[i], near_recv.at[i], device)

    mine = [x * (blocks // 2) + c * (blocks // 4) + i for i in range(blocks // 4)]
    theirs = [(1 - x) * (blocks // 2) + c * (blocks // 4) + i for i in range(blocks // 4)]
    band_x = [near(16 + i, band_source(block), band.at[block], to_x) for i, block in enumerate(mine)]
    tok_x = near(1, inputs_ref.at[1 - x, pl.ds(c * quarter, quarter)], tok.at[x_rows(x, c)], to_x)
    cot_x = near(2, cots_ref.at[1 - x, pl.ds(c * quarter, quarter)], cot.at[x_rows(x, c)], to_x)
    band_c = [near(16 + len(mine) + i, band.at[block], band.at[block], to_c) for i, block in enumerate(theirs)]
    tok_c = near(4, tok.at[x_rows(1 - x, c)], tok.at[x_rows(1 - x, c)], to_c)
    cot_c = near(5, cot.at[x_rows(1 - x, c)], cot.at[x_rows(1 - x, c)], to_c)
    for copy in band_x:
        copy.start()
    tok_x.start()
    gather.plan(window)
    cot_x.start()
    own_full.wait()
    lanes_of = lax.broadcasted_iota(jnp.int32, (length, 128), 1)
    rows_of = lax.broadcasted_iota(jnp.int32, (length, 128), 0)
    valid = lengths_ref[x, 0]
    blocked = jnp.where(rows_of // BLOCK == lanes_of, 1.0, 0.0)
    kaux[...] = jnp.where((lanes_of == blocks) & (rows_of >= valid), -1e30, blocked).astype(low)
    for copy in band_x:
        copy.wait()
    for copy in band_c:
        copy.start()
    tok_x.wait()
    tok_c.start()
    for copy in (*own_bands, *band_c):
        copy.wait()
    gather.run(2)

    def bias_step(i, carry):
        block = i // (BLOCK // 16)
        at = pl.multiple_of((i % (BLOCK // 16)) * 16, 16)
        index = band[block, pl.ds(at, 16), :]
        for col in range(BAND):
            lanes = slice(col * BLOCK, (col + 1) * BLOCK)
            for head in range(heads):
                table = table_ref[head]
                got = [jnp.take_along_axis(table, index[8 * k : 8 * k + 8, lanes], axis=1) for k in range(2)]
                bias[head, block, pl.ds(at, 16), lanes] = jnp.concatenate(got, axis=0).astype(low)
        return carry

    lax.fori_loop(0, blocks * (BLOCK // 16) // 2, bias_step, 0)
    gather.run(4)
    lax.fori_loop(blocks * (BLOCK // 16) // 2, blocks * (BLOCK // 16), bias_step, 0)
    gather.run(2)

    def biast_store(block, slot):
        return pltpu.make_async_copy(biast.at[slot], biast_out.at[:, block], bt_sem.at[slot])

    def biast_block(block, carry):
        slot = block % 2

        @pl.when(block > 1)
        def _():
            biast_store(block - 2, slot).wait()

        bandt[block] = jnp.transpose(band[block].astype(jnp.float32)).astype(low)

        def inner_step(i, carry):
            at = pl.multiple_of(i * 16, 16)
            index = bandt[block, pl.ds(at, 16), :].astype(jnp.float32).astype(jnp.int32)
            for head in range(heads):
                got = [jnp.take_along_axis(table_ref[head], index[8 * k : 8 * k + 8], axis=1) for k in range(2)]
                biast[slot, head, pl.ds(at, 16), :] = jnp.concatenate(got, axis=0).astype(low)
            return carry

        lax.fori_loop(0, BAND * BLOCK // 16, inner_step, 0)
        biast_store(block, slot).start()
        return carry

    lax.fori_loop(0, blocks // 2, biast_block, 0)
    gather.run(4)
    lax.fori_loop(blocks // 2, blocks, biast_block, 0)
    gather.run(2)
    biast_store(blocks - 2, 0).wait()
    biast_store(blocks - 1, 1).wait()
    bandt_store = own_load(4, bandt, bandt_out)
    bandt_store.start()
    own_tok.wait()
    tok_c.wait()
    own_cot.wait()
    cot_x.wait()
    cot_c.start()
    cot_c.wait()

    def live_step(i, carry):
        rows = pl.ds(pl.multiple_of(i * BLOCK, BLOCK), BLOCK)
        here = lax.broadcasted_iota(jnp.int32, (BLOCK, width), 0) + i * BLOCK < valid
        masked = jnp.where(here, cot[rows, :].astype(jnp.float32), 0.0).astype(low)
        cot[rows, :] = masked
        low_t[:, rows] = jnp.transpose(masked)
        return carry

    lax.fori_loop(0, blocks, live_step, 0)

    gather.need(qkv_pieces)
    load_gains = own_load(5, full_ref.at[:, :, :, :, 0:at_q], gain_buf)
    third = 3 * inner // 2
    loads_wide = [
        pltpu.make_async_copy(
            full_ref.at[:, :, :, :, at_q + third * k : at_q + third * (k + 1)], w_buf.at[k, :, :, :, :, 0:third], w_sem.at[k]
        )
        for k in range(2)
    ]
    for copy in (load_gains, *loads_wide):
        copy.start()
    load_gains.wait()
    gains = jnp.transpose(gain_buf[...].reshape(width, 128).astype(jnp.float32))
    gain_one, gain_two = gains[0:1, :], gains[1:2, :]

    def norm_step(i, carry):
        rows = pl.ds(pl.multiple_of(i * BLOCK, BLOCK), BLOCK)
        present = tok[rows, :].astype(jnp.float32)
        inverse = lax.rsqrt(jnp.mean(present * present, axis=-1, keepdims=True) + EPSILON)
        got = (present * inverse * gain_one).astype(low)
        normed[rows, :] = got
        two_t[:, rows] = jnp.transpose(got)
        return carry

    lax.fori_loop(0, blocks, norm_step, 0)
    normed_store = own_load(6, two_t, normed_out)
    normed_store.start()
    for copy in loads_wide:
        copy.wait()
    gather.run(2)

    for col in range(3 * pairs // 2):
        slot, at = 256 * col // third, 256 * col % third
        lanes = slice(at, at + 256)

        def qkv_step(i, carry):
            rows = pl.ds(pl.multiple_of(i * 256, 256), 256)
            got = jnp.dot(
                normed[rows, :], w_buf[slot, :, :, :, :, lanes].reshape(width, 256), preferred_element_type=jnp.float32
            ).astype(low)
            qkv[2 * col, rows, :] = got[:, :128]
            qkv[2 * col + 1, rows, :] = got[:, 128:]
            return carry

        lax.fori_loop(0, length // 256, qkv_step, 0)
        if col % 2:
            gather.run(1)
    qkv_store = own_load(7, qkv, qkv_out)
    qkv_store.start()

    units = pairs * (length // 256)
    acts = gather.take(min(len(gather.queue), 10))

    def unit_step(unit, carry):
        for k, act in enumerate(acts):
            @pl.when(unit == (k * units) // len(acts))
            def _(act=act):
                act()
        pair = unit // (length // 256)
        step = unit % (length // 256)
        rows = pl.ds(pl.multiple_of(step * 256, 256), 256)
        queries = qkv[pair, rows, :]
        keys = jnp.concatenate([qkv[pairs + pair], kaux[...]], axis=1)
        outs = []
        for head in range(2):
            aux = query_aux(table_ref[2 * pair + head], step, blocks)
            masked = jnp.where(lane_head(256, 128, head), queries, jnp.zeros_like(queries))
            scores[...] = lax.dot_general(
                jnp.concatenate([masked, aux], axis=1), keys, LAST, preferred_element_type=jnp.float32
            )
            for sub in range(2):
                start = pl.multiple_of(band_start(step * 2 + sub, blocks) * BLOCK, BLOCK)
                scores[sub * BLOCK : (sub + 1) * BLOCK, pl.ds(start, BAND * BLOCK)] += bias[
                    2 * pair + head, 2 * step + sub
                ].astype(jnp.float32)
            got = scores[...]
            highest = jnp.max(got, axis=1, keepdims=True)
            exponent = jnp.exp(got - highest)
            total = jnp.sum(exponent, axis=1, keepdims=True)
            outs.append(
                jnp.dot(exponent.astype(low), qkv[2 * pairs + pair], preferred_element_type=jnp.float32) * (1.0 / total)
            )
            lse = jnp.broadcast_to(highest + jnp.log(total), (256, 128))
            lse_ref[pair, step, head : head + 1, :] = jnp.transpose(lse)[0:1, :]
        attended[pair, rows, :] = jnp.where(lane_head(256, 128, 0), outs[0], outs[1]).astype(low)
        return carry

    lax.fori_loop(0, units, unit_step, 0)
    normed_store.wait()
    two = normed
    gather.need(project_pieces)
    load_project = own_load(9, full_ref.at[:, :, :, :, at_project:at_hidden], project_w)
    load_project.start()
    load_project.wait()

    def branch(rows):
        left = jnp.concatenate([attended[pair, rows, :] for pair in range(pairs)], axis=1)
        return lax.dot_general(left, project_w[...].reshape(width, inner), LAST, preferred_element_type=jnp.float32)

    def part_rows(part, core):
        return pl.ds(pl.multiple_of(part * half + core * quarter, quarter), quarter)

    def swap_part(i, part, slot=0):
        return near(i + part, away.at[slot + part], arrived.at[slot + part], to_c)

    for part in range(2):
        away[part] = branch(part_rows(part, 1 - c)).astype(low)
        swap_part(6, part).start()
    for part in range(2):
        normal[part] = branch(part_rows(part, c)) + tok[part_rows(part, c), :].astype(jnp.float32)

    def share(i, part, buffer):
        return near(i + part, buffer.at[part_rows(part, c)], buffer.at[part_rows(part, c)], to_c)

    tokens_store = [own_load(11 + part, tok.at[part_rows(part, c)], tokens_own_ref.at[part]) for part in range(2)]
    for copy in tokens_store:
        copy.start()
    for part in range(2):
        swap_part(6, part).wait()
        middle = normal[part] + arrived[part].astype(jnp.float32)
        normal[part] = middle
        inverse = lax.rsqrt(jnp.mean(middle * middle, axis=-1, keepdims=True) + EPSILON)
        two[part_rows(part, c), :] = (middle * inverse * gain_two).astype(low)
        share(8, part, two).start()
    gather.run(2)
    for part in range(2):
        share(8, part, two).wait()

    def turn_step(i, carry):
        rows = pl.ds(pl.multiple_of(i * BLOCK, BLOCK), BLOCK)
        two_t[:, rows] = jnp.transpose(two[rows, :])
        return carry

    lax.fori_loop(0, blocks, turn_step, 0)
    gather.run(2)

    def bounds(j):
        at = at_hidden + 3 * HIDDEN_STEP * j
        return at, at + 3 * steps[j]

    def load_step(j):
        a, b = bounds(j)
        return pltpu.make_async_copy(
            full_ref.at[:, :, :, :, a:b], w_buf.at[j % 2, :, :, :, :, 0 : b - a], w_sem.at[j % 2]
        )

    def store_step(j):
        a, b = bounds(j)
        return pltpu.make_async_copy(
            g_buf.at[j % 2, :, :, :, :, 0 : b - a],
            grads_out.at[:, :, :, :, a - at_hidden : b - at_hidden],
            g_sem.at[j % 2],
        )

    gather.need(range(first_hidden_piece, first_hidden_piece + per_step))
    load_step(0).start()
    for j, units_here in enumerate(steps):
        n = units_here
        slot = j % 2
        load_step(j).wait()

        def weight(k, slot=slot, n=n):
            return w_buf[slot, :, :, :, :, k * n : (k + 1) * n].reshape(width, n)

        def rows_step(i, carry, j=j, n=n, weight=weight):
            rows = pl.ds(pl.multiple_of(i * 256, 256), 256)
            left, grad = two[rows, :], cot[rows, :]
            gate = jnp.dot(left, weight(0), preferred_element_type=jnp.float32)
            up = jnp.dot(left, weight(1), preferred_element_type=jnp.float32)
            grad_hidden = jnp.dot(grad, weight(2), preferred_element_type=jnp.float32)
            value, slope = gelu_all(gate)
            hid[rows, 0:n] = (value * up).astype(low)
            ggate[rows, 0:n] = (grad_hidden * up * slope).astype(low)
            gup[rows, 0:n] = (grad_hidden * value).astype(low)
            out = lax.dot_general(hid[rows, 0:n], weight(2), LAST, preferred_element_type=jnp.float32)
            back = lax.dot_general(ggate[rows, 0:n], weight(0), LAST, preferred_element_type=jnp.float32)
            back = back + lax.dot_general(gup[rows, 0:n], weight(1), LAST, preferred_element_type=jnp.float32)
            if j == 0:
                acc_out[rows, :] = out
                acc_two[rows, :] = back
            else:
                acc_out[rows, :] += out
                acc_two[rows, :] += back
            return carry

        lax.fori_loop(0, length // 256, rows_step, 0)
        gather.run(2)
        if j + 1 < len(steps):
            first = first_hidden_piece + per_step * (j + 1)
            gather.need(range(first, first + per_step))
            load_step(j + 1).start()
        if j > 1:
            store_step(j - 2).wait()

        tiles = width // 256

        def grads_step(i, carry, slot=slot, n=n):
            rows = pl.ds(pl.multiple_of(i * 256, 256), 256)
            for k, (left, right) in enumerate(((two_t, ggate), (two_t, gup), (low_t, hid))):
                got = jnp.dot(left[rows, :], right[:, 0:n], preferred_element_type=jnp.float32).astype(low)
                span = deep // tiles
                g_buf[slot, pl.ds(i * span, span), :, :, :, k * n : (k + 1) * n] = got.reshape(
                    (span,) + g_buf.shape[2:5] + (n,)
                )
            return carry

        lax.fori_loop(0, tiles, grads_step, 0)
        store_step(j).start()
    gather.run(len(gather.queue))

    def share_sum(i, acc, slot):
        for part in range(2):
            away[slot + part] = acc[part_rows(part, 1 - c), :].astype(low)
            swap_part(i, part, slot).start()

    share_sum(10, acc_two, 0)
    for part in range(2):
        swap_part(10, part).wait()
        grad_two = acc_two[part_rows(part, c), :] + arrived[part].astype(jnp.float32)
        middle = normal[part]
        inverse = lax.rsqrt(jnp.mean(middle * middle, axis=-1, keepdims=True) + EPSILON)
        unit = middle * inverse
        weighted = jnp.sum((grad_two * unit).reshape(quarter // 8, 8, width), axis=0)
        gain_ref[part] = weighted
        scaled = grad_two * gain_two
        grad_middle = cot[part_rows(part, c), :].astype(jnp.float32) + inverse * (
            scaled - unit * jnp.mean(scaled * unit, axis=-1, keepdims=True)
        )
        middle_grad_ref[part] = grad_middle
        two[part_rows(part, c), :] = grad_middle.astype(low)
        share(12, part, two).start()
    share_sum(14, acc_out, 2)
    for part in range(2):
        swap_part(14, part, 2).wait()
        output_ref[part] = (normal[part] + acc_out[part_rows(part, c), :] + arrived[2 + part].astype(jnp.float32)).astype(low)
    for part in range(2):
        share(12, part, two).wait()
    for j in range(max(0, len(steps) - 2), len(steps)):
        store_step(j).wait()

    lax.fori_loop(0, blocks, turn_step, 0)

    def project_step(i, carry):
        rows = pl.ds(pl.multiple_of(i * 256, 256), 256)
        right = jnp.concatenate([attended[pair] for pair in range(pairs)], axis=1)
        got = jnp.dot(two_t[rows, :], right, preferred_element_type=jnp.float32).astype(low)
        span = deep // (width // 256)
        g_buf[0, pl.ds(i * span, span), :, :, :, 0:inner] = got.reshape((span,) + g_buf.shape[2:5] + (inner,))
        return carry

    lax.fori_loop(0, width // 256, project_step, 0)
    project_store = own_load(8, g_buf.at[0, :, :, :, :, 0:inner], grads_out.at[:, :, :, :, 3 * hidden : 3 * hidden + inner])
    project_store.start()

    def attended_step(i, carry):
        rows = pl.ds(pl.multiple_of(i * 256, 256), 256)
        got = jnp.dot(two[rows, :], project_w[...].reshape(width, inner), preferred_element_type=jnp.float32).astype(low)
        for pair in range(pairs):
            attended[pair, rows, :] = got[:, pair * 128 : (pair + 1) * 128]
        return carry

    lax.fori_loop(0, length // 256, attended_step, 0)
    attended_store = own_load(10, attended, attended_out)
    attended_store.start()
    for copy in (bandt_store, qkv_store, attended_store, project_store, *tokens_store):
        copy.wait()
    gather.sent()


def front(shard_size, pieces, window, lengths, gains, weights, inputs, cots, buckets, table_rows):
    low, f32 = jnp.bfloat16, jnp.float32
    deep = shard_size // 2
    rows, inner = weights[0].shape
    hidden = weights[4].shape[1]
    wide = pieces[-1][1]
    half, width = inputs.shape[1:]
    length, quarter = 2 * half, half // 2
    heads = table_rows.shape[0]
    blocks = length // BLOCK
    pairs = heads // 2
    shape = jax.ShapeDtypeStruct
    vmem, hbm = pl.BlockSpec(memory_space=pltpu.VMEM), pl.BlockSpec(memory_space=pl.ANY)
    dma = pltpu.SemaphoreType.DMA
    count = len(pieces)
    step = HIDDEN_STEP
    out_shape = [
        shape((deep, 2, 2, rows, wide), low),
        shape((width, length), low),
        shape((3 * pairs, length, 128), low),
        shape((blocks, BAND * BLOCK, BLOCK), low),
        shape((heads, blocks, BAND * BLOCK, BLOCK), low),
        shape((deep, 2, 2, rows, 3 * hidden + inner), low),
        shape((pairs, length, 128), low),
        shape((2, quarter, width), low),
        shape((pairs, length // 256, 2, 256), f32),
        shape((2, quarter, width), low),
        shape((2, quarter, width), f32),
        shape((2, 8, width), f32),
    ]
    scratch = [
        pltpu.VMEM((rows, wide), low),
        pltpu.VMEM((length, width), low),
        pltpu.VMEM((length, width), low),
        pltpu.VMEM((blocks, BLOCK, BAND * BLOCK), jnp.int32),
        pltpu.VMEM((blocks, BAND * BLOCK, BLOCK), low),
        pltpu.VMEM((heads, blocks, BLOCK, BAND * BLOCK), low),
        pltpu.VMEM((2, heads, BAND * BLOCK, BLOCK), low),
        pltpu.VMEM((length, 128), low),
        pltpu.VMEM((deep, 2, 2, rows, 128), low),
        pltpu.VMEM((3 * pairs, length, 128), low),
        pltpu.VMEM((length, width), low),
        pltpu.VMEM((256, length), f32),
        pltpu.VMEM((pairs, length, 128), low),
        pltpu.VMEM((deep, 2, 2, rows, inner), low),
        pltpu.VMEM((2, quarter, width), f32),
        pltpu.VMEM((4, quarter, width), low),
        pltpu.VMEM((4, quarter, width), low),
        pltpu.VMEM((width, length), low),
        pltpu.VMEM((width, length), low),
        pltpu.VMEM((length, width), f32),
        pltpu.VMEM((length, width), f32),
        pltpu.VMEM((2, deep, 2, 2, rows, 3 * step), low),
        pltpu.VMEM((2, deep, 2, 2, rows, 3 * step), low),
        pltpu.VMEM((length, step), low),
        pltpu.VMEM((length, step), low),
        pltpu.VMEM((length, step), low),
        dma((count, 3, deep - 1)),
        dma((count, 3, deep - 1)),
        dma((16 + blocks // 2,)),
        dma((16 + blocks // 2,)),
        dma((13 + blocks // 2,)),
        dma((2,)),
        dma((2,)),
        dma((5 + 3 * len(hidden_steps(hidden)),)),
        dma((2,)),
    ]
    return pl.pallas_call(
        functools.partial(front_kernel, shard_size, pieces, window, (inner, hidden)),
        out_shape=out_shape,
        in_specs=[pl.BlockSpec(memory_space=pltpu.SMEM)] + [hbm] * 11 + [vmem],
        out_specs=[hbm] * 8 + [vmem] * 4,
        scratch_shapes=scratch,
        compiler_params=pltpu.CompilerParams(
            collective_id=1, has_side_effects=True, vmem_limit_bytes=60 * MIB
        ),
        name="front",
    )(lengths, gains, *weights, inputs, cots, buckets, table_rows)


GROUP = 16
TURNS = 4


class Scatter:
    def __init__(self, place, pieces, sources, outs, buffers, sems):
        self.place, self.pieces, self.sources, self.outs = place, pieces, sources, outs
        self.first, self.own, self.second, self.third = buffers
        self.own_sem, self.send_sem, self.recv_sem = sems
        self.queue = []

    def peer(self, name):
        place = self.place
        return place.device(y=1 - place.y) if name == "y" else place.device(x=1 - place.x)

    def rest(self, piece):
        order = self.pieces[piece][3]
        return [name for name in "zyx" if name != order[0]]

    def cut(self, piece, name, value):
        t, a, b, _ = self.pieces[piece]
        at = [value if name == other else slice(None) for other in "zyx"]
        return self.sources[t].at[at[0], at[1], at[2], :, a:b]

    def own_copy(self, piece):
        order = self.pieces[piece][3]
        return pltpu.make_async_copy(
            self.cut(piece, order[0], getattr(self.place, order[0])), self.own[piece], self.own_sem.at[piece]
        )

    def copies(self, piece, hop):
        place, order = self.place, self.pieces[piece][3]
        name, rest = order[hop], self.rest(piece)
        own, made = self.own[piece], []

        def at(**index):
            return tuple(index[n] if n in index else slice(None) for n in rest)

        def add(source, target, device):
            i = len(made)
            made.append(send(source, target, self.send_sem.at[piece, hop, i], self.recv_sem.at[piece, hop, i], device))

        if hop == 0:
            if name == "z":
                for d in range(1, place.deep):
                    z = place.line(d)
                    add(self.cut(piece, "z", z), self.first[piece].at[d - 1], place.device(z=z))
            else:
                add(self.cut(piece, name, 1 - getattr(place, name)), self.first[piece], self.peer(name))
            return made
        fixed = {} if hop == 1 else {order[1]: getattr(place, order[1])}
        buffer = self.second[piece] if hop == 1 else self.third[piece]
        if name == "z":
            for d in range(1, place.deep):
                z = place.line(d)
                add(own.at[at(z=z, **fixed)], buffer.at[d - 1], place.device(z=z))
        else:
            add(own.at[at(**{name: 1 - getattr(place, name)}, **fixed)], buffer, self.peer(name))
        return made

    def start(self, piece, hop):
        for copy in self.copies(piece, hop):
            copy.start()

    def arrive(self, piece, hop):
        for copy in self.copies(piece, hop):
            copy.wait_recv()

    def begin(self, pieces):
        for piece in pieces:
            self.start(piece, 0)
            self.own_copy(piece).start()

    def add_first(self, piece):
        order = self.pieces[piece][3]
        self.arrive(piece, 0)
        self.own_copy(piece).wait()
        own, came = self.own[piece], self.first[piece]
        inner = own.shape[1]

        def body(i, carry):
            for k in range(inner):
                if order[0] == "z":
                    total = own[i, k].astype(jnp.float32)
                    for d in range(came.shape[0]):
                        total = total + came[d, i, k].astype(jnp.float32)
                    own[i, k] = total.astype(jnp.bfloat16)
                else:
                    own[i, k] = own[i, k] + came[i, k]
            return carry

        lax.fori_loop(0, own.shape[0], body, 0)
        self.start(piece, 1)

    def add_second(self, piece):
        place, order = self.place, self.pieces[piece][3]
        name, rest = order[1], self.rest(piece)
        self.arrive(piece, 1)
        own, came = self.own[piece], self.second[piece]
        mine = getattr(place, name)
        spans = own.shape[1] if rest[0] == name else own.shape[0]

        def body(i, carry):
            if rest[0] == name:
                own[mine, i] = own[mine, i] + came[i]
            else:
                own[i, mine] = own[i, mine] + came[i]
            return carry

        lax.fori_loop(0, spans, body, 0)
        self.start(piece, 2)

    def add_third(self, piece):
        place, order = self.place, self.pieces[piece][3]
        t, a, b, _ = self.pieces[piece]
        rest = self.rest(piece)
        self.arrive(piece, 2)
        total = self.own[piece][getattr(place, rest[0]), getattr(place, rest[1])].astype(jnp.float32)
        if order[2] == "z":
            for d in range(1, place.deep):
                total = total + self.third[piece][d - 1].astype(jnp.float32)
        else:
            total = total + self.third[piece][...].astype(jnp.float32)
        self.outs[t][:, a:b] = total

    def plan(self, pieces):
        pieces = list(pieces)
        for i in range(len(pieces) + 2):
            if i < len(pieces):
                self.queue.append(functools.partial(self.add_first, pieces[i]))
            if 0 < i <= len(pieces):
                self.queue.append(functools.partial(self.add_second, pieces[i - 1]))
            if i > 1:
                self.queue.append(functools.partial(self.add_third, pieces[i - 2]))

    def run(self, steps):
        for _ in range(min(steps, len(self.queue))):
            self.queue.pop(0)()

    def take(self, steps):
        taken, self.queue = self.queue[:steps], self.queue[steps:]
        return taken

    def sent(self):
        for piece in range(len(self.pieces)):
            for hop in range(3):
                for copy in self.copies(piece, hop):
                    copy.wait_send()


def piece_buffers(piece, deep, rows):
    _, a, b, order = piece
    sizes = {"z": deep, "y": 2, "x": 2}
    rest = [name for name in "zyx" if name != order[0]]
    left = [sizes[name] for name in rest]
    last = [sizes[name] for name in rest if name != order[1]]
    tail = [rows, b - a]
    lead = [deep - 1]
    first = (lead if order[0] == "z" else []) + left + tail
    second = (lead if order[1] == "z" else []) + last + tail
    third = (lead if order[2] == "z" else []) + tail
    return [tuple(shape) for shape in (first, left + tail, second, third)]


def back_kernel(shard_size, pieces, early, sizes, *refs):
    inner, hidden, buckets = sizes
    count = len(pieces)
    (
        lengths_ref, full_ref, normed_in, qkv_in, bandt_in, biast_in, grads_in, do_in,
        lse_ref, output_ref, middle_ref, tokens_ref, gain_two_ref, table_ref,
    ) = refs[:14]
    refs = refs[14:]
    hidden_out, weight_sums, output_out, input_out, small_out = refs[:5]
    refs = refs[5:]
    first, own, second, third = [refs[k * count : (k + 1) * count] for k in range(4)]
    refs = refs[4 * count :]
    (
        qkv, normed_t, bandt, bias, wqkv, gain_buf, do, scores, grads, far, dk_acc, dv_acc, kaux, wgrad,
        mine_sum, away, arrived, result, table_acc, hot, found,
        small, small_x, small_y, hold_x, hold_y, hold_z, small_c,
        own_sem, send_sem, recv_sem, near_send, near_recv, local_sem,
    ) = refs
    length = qkv.shape[1]
    width = normed_t.shape[0]
    half, quarter = length // 2, length // 4
    heads, blocks = bias.shape[:2]
    pairs = heads // 2
    deep = shard_size // 2
    low, f32 = jnp.bfloat16, jnp.float32
    place = Place(shard_size)
    x, y, z, c = place.x, place.y, place.z, place.c
    to_x, to_y, to_c = place.device(x=1 - x), place.device(y=1 - y), place.device(c=1 - c)

    def local(i, source, target):
        return pltpu.make_async_copy(source, target, local_sem.at[i])

    loads = [
        local(0, qkv_in, qkv), local(1, biast_in, bias), local(2, do_in, do),
        local(3, full_ref.at[:, :, :, :, 128 : 128 + 3 * inner], wqkv), local(4, normed_in, normed_t),
        local(5, bandt_in, bandt), local(6, full_ref.at[:, :, :, :, 0:128], gain_buf),
    ]
    for copy in loads:
        copy.start()
    meet(place)
    scatter = Scatter(
        place, pieces, (grads_in, wgrad), (hidden_out, weight_sums), (first, own, second, third), (own_sem, send_sem, recv_sem),
    )
    scatter.begin(range(early))
    scatter.plan(range(early))

    def near(i, source, target, device):
        return send(source, target, near_send.at[i], near_recv.at[i], device)

    def to_owners(i, values, out):
        here = out.at[x, pl.ds(c * quarter, quarter)]
        there = out.at[1 - x, pl.ds(c * quarter, quarter)]
        return (
            local(7 + i, values.at[x], here),
            near(4 * i, values.at[x], here, to_c),
            near(4 * i + 1, values.at[1 - x], here, to_x),
            near(4 * i + 2, there, there, to_c),
        )

    output_moves = to_owners(0, output_ref, output_out)
    for copy in output_moves[:3]:
        copy.start()

    lanes_of = lax.broadcasted_iota(jnp.int32, (length, 128), 1)
    rows_of = lax.broadcasted_iota(jnp.int32, (length, 128), 0)
    valid = lengths_ref[x, 0]
    blocked = jnp.where(rows_of // BLOCK == lanes_of, 1.0, 0.0)
    kaux[...] = jnp.where((lanes_of == blocks) & (rows_of >= valid), -1e30, blocked).astype(low)
    far[...] = jnp.zeros_like(far)
    for copy in loads[:3]:
        copy.wait()

    per_pair = length // 256
    units = pairs * per_pair
    acts = scatter.take(ATTENTION_ACTS)

    def unit_step(unit, carry):
        for k, act in enumerate(acts):
            @pl.when(unit == (k * units) // len(acts))
            def _(act=act):
                act()
        pair = unit // per_pair
        step = unit % per_pair
        rows = pl.ds(pl.multiple_of(step * 256, 256), 256)

        @pl.when(step == 0)
        def _():
            dk_acc[...] = jnp.zeros_like(dk_acc)
            dv_acc[...] = jnp.zeros_like(dv_acc)

        queries = qkv[pair, rows, :]
        grad = do[pair, rows, :]
        key_pair = qkv[pairs + pair]
        keys = jnp.concatenate([key_pair, kaux[...]], axis=1)
        values = qkv[2 * pairs + pair]
        dq = None
        for head in range(2):
            here = lane_head(256, 128, head)
            aux = query_aux(table_ref[2 * pair + head], step, blocks)
            q_masked = jnp.where(here, queries, jnp.zeros_like(queries))
            do_masked = jnp.where(here, grad, jnp.zeros_like(grad))
            scores[...] = lax.dot_general(
                keys, jnp.concatenate([q_masked, aux], axis=1), LAST, preferred_element_type=f32
            )
            for sub in range(2):
                start = pl.multiple_of(band_start(step * 2 + sub, blocks) * BLOCK, BLOCK)
                scores[pl.ds(start, BAND * BLOCK), sub * BLOCK : (sub + 1) * BLOCK] += bias[
                    2 * pair + head, 2 * step + sub
                ].astype(f32)
            soft = jnp.exp(scores[...] - lse_ref[pair, step, head : head + 1, :])
            dv_acc[...] += jnp.dot(soft.astype(low), do_masked, preferred_element_type=f32)
            grad_probs = lax.dot_general(values, do_masked, LAST, preferred_element_type=f32)
            weighted = jnp.sum(soft * grad_probs, axis=0, keepdims=True)
            grad_scores = (soft * (grad_probs - weighted)).astype(low)
            grads[...] = grad_scores
            dk_acc[...] += jnp.dot(grad_scores, q_masked, preferred_element_type=f32)
            k_masked = jnp.where(lane_head(length, 128, head), key_pair, jnp.zeros_like(key_pair))
            part = lax.dot_general(grad_scores, k_masked, FIRST, preferred_element_type=f32)
            dq = part if dq is None else dq + part
            sums = jnp.concatenate(
                [
                    jnp.sum(grad_scores[block * BLOCK : (block + 1) * BLOCK, :].astype(f32), axis=0, keepdims=True)
                    for block in range(blocks)
                ],
                axis=0,
            )
            block_of = lax.broadcasted_iota(jnp.int32, (blocks, BLOCK), 0)
            for sub in range(2):
                start = band_start(step * 2 + sub, blocks)
                at = pl.multiple_of(start * BLOCK, BLOCK)
                bias[2 * pair + head, 2 * step + sub] = grads[pl.ds(at, BAND * BLOCK), sub * BLOCK : (sub + 1) * BLOCK]
                part = sums[:, sub * BLOCK : (sub + 1) * BLOCK]
                far[0, 2 * pair + head] += jnp.where(block_of < start, part, 0.0)
                far[1, 2 * pair + head] += jnp.where(block_of >= start + BAND, part, 0.0)
        qkv[pair, rows, :] = dq.astype(low)

        @pl.when(step == per_pair - 1)
        def _():
            qkv[pairs + pair] = dk_acc[...].astype(low)
            qkv[2 * pairs + pair] = dv_acc[...].astype(low)

        return carry

    lax.fori_loop(0, units, unit_step, 0)
    for copy in output_moves[:3]:
        copy.wait()
    output_moves[3].start()
    for copy in loads[3:]:
        copy.wait()

    for t in range(3):
        def weight_step(i, carry, t=t):
            rows = pl.ds(pl.multiple_of(i * 256, 256), 256)
            right = jnp.concatenate([qkv[t * pairs + pair] for pair in range(pairs)], axis=1)
            got = jnp.dot(normed_t[rows, :], right, preferred_element_type=f32).astype(low)
            span = deep // (width // 256)
            wgrad[pl.ds(i * span, span), :, :, :, t * inner : (t + 1) * inner] = got.reshape(
                (span,) + wgrad.shape[1:4] + (inner,)
            )
            return carry

        lax.fori_loop(0, width // 256, weight_step, 0)
        late = [i for i in range(early, count) if t * inner <= pieces[i][1] < (t + 1) * inner]
        scatter.begin(late)
        scatter.plan(late)
        scatter.run(2)

    def part_rows(part, core):
        return pl.ds(pl.multiple_of(part * half + core * quarter, quarter), quarter)

    def grad_one(rows):
        left = jnp.concatenate([qkv[k, rows, :] for k in range(3 * pairs)], axis=1)
        return lax.dot_general(left, wqkv[...].reshape(width, 3 * inner), LAST, preferred_element_type=f32)

    swaps = [near(8 + part, away.at[part], arrived.at[part], to_c) for part in range(2)]

    def away_step(part, carry):
        away[part] = grad_one(part_rows(part, 1 - c)).astype(low)
        return carry

    def mine_step(part, carry):
        mine_sum[part] = grad_one(part_rows(part, c))
        return carry

    lax.fori_loop(0, 2, away_step, 0)
    for copy in swaps:
        copy.start()
    lax.fori_loop(0, 2, mine_step, 0)
    gains = jnp.transpose(gain_buf[...].reshape(width, 128).astype(f32))
    gain_one = gains[0:1, :]
    gain_sum = jnp.zeros((1, width), f32)
    for part in range(2):
        swaps[part].wait()
        total = mine_sum[part] + arrived[part].astype(f32)
        present = tokens_ref[part].astype(f32)
        inverse = lax.rsqrt(jnp.mean(present * present, axis=-1, keepdims=True) + EPSILON)
        unit = present * inverse
        gain_sum = gain_sum + jnp.sum(total * unit, axis=0, keepdims=True)
        scaled = total * gain_one
        back = inverse * (scaled - unit * jnp.mean(scaled * unit, axis=-1, keepdims=True))
        result[part] = (middle_ref[part] + back).astype(low)
    input_moves = to_owners(1, result, input_out)
    for copy in input_moves[:3]:
        copy.start()
    scatter.run(2)

    table_acc[...] = jnp.zeros_like(table_acc)
    groups = BAND * BLOCK // GROUP
    table_units = blocks // 2 * groups // TURNS
    table_acts = scatter.take(len(scatter.queue))

    def table_step(i, carry):
        for k, act in enumerate(table_acts):
            @pl.when(i == (k * table_units) // max(1, len(table_acts)))
            def _(act=act):
                act()
        total = None
        for turn in range(TURNS):
            group = i * TURNS + turn
            block = 2 * (group // groups)
            start = pl.multiple_of((group % groups) * GROUP, GROUP)
            for two in range(2):
                lanes = slice(two * BLOCK, (two + 1) * BLOCK)
                index = bandt[block + two, pl.ds(start, GROUP), :]
                for head in range(heads):
                    found[turn, head * GROUP : (head + 1) * GROUP, lanes] = bias[head, block + two, pl.ds(start, GROUP), :]
                for b in range(buckets):
                    hot[turn, b * GROUP : (b + 1) * GROUP, lanes] = jnp.where(
                        index == jnp.asarray(b, low), jnp.asarray(1, low), jnp.asarray(0, low)
                    )
            part = lax.dot_general(hot[turn], found[turn], LAST, preferred_element_type=f32)
            total = part if total is None else total + part
        table_acc[...] += total
        return carry

    lax.fori_loop(0, table_units, table_step, 0)
    row = lax.broadcasted_iota(jnp.int32, table_acc.shape, 0) % GROUP
    col = lax.broadcasted_iota(jnp.int32, table_acc.shape, 1) % GROUP
    kept = jnp.where(row == col, table_acc[...], 0.0).reshape(buckets, GROUP, heads * GROUP).sum(axis=1)
    bucket = lax.broadcasted_iota(jnp.int32, (buckets, 128), 0)
    head_of = lax.broadcasted_iota(jnp.int32, (buckets, 128), 1)
    table = jnp.zeros((buckets, 128), f32)
    for head in range(heads):
        amount = jnp.sum(kept[:, head * GROUP : (head + 1) * GROUP], axis=1, keepdims=True)
        table = table + jnp.where(head_of == head, amount, 0.0)
    for side, name in enumerate((buckets // 2 - 1, buckets - 1)):
        for head in range(heads):
            amount = jnp.sum(jnp.sum(far[side, head], axis=0, keepdims=True), axis=1, keepdims=True)
            table = table + jnp.where((bucket == name) & (head_of == head), amount, 0.0)

    lines = width // 128
    for i in range(lines):
        small[i : i + 1, :] = gain_sum[:, i * 128 : (i + 1) * 128]
    small[lines : 2 * lines, :] = gain_two_ref[...]
    small[2 * lines : 2 * lines + buckets, :] = table
    small_base = 10

    def small_line(d):
        return near(small_base + 2 + d, hold_z.at[z], hold_z.at[z], place.device(z=place.line(d)))

    move = near(small_base, small, small_x, to_x)
    move.start()
    move.wait()
    hold_x[...] = small[...] + small_x[...]
    move = near(small_base + 1, hold_x, small_y, to_y)
    move.start()
    move.wait()
    hold_z[z] = hold_x[...] + small_y[...]
    for d in range(1, deep):
        small_line(d).start()
    for d in range(1, deep):
        small_line(d).wait()
    hold_y[...] = jnp.sum(hold_z[...], axis=0)
    move = near(small_base + 2, hold_y, small_c, to_c)
    move.start()
    move.wait()
    small_out[0] = hold_y[...]
    small_out[1] = hold_y[...] + small_c[...]

    for copy in input_moves[:3]:
        copy.wait()
    input_moves[3].start()
    input_moves[3].wait()
    output_moves[3].wait()
    scatter.run(len(scatter.queue))
    scatter.sent()


def back(shard_size, pieces, early, buckets, lengths, full, normed_t, qkv, bandt, biast, grads, do, lse, output, middle, tokens, gain_two, table_rows):
    low, f32 = jnp.bfloat16, jnp.float32
    deep = shard_size // 2
    rows = full.shape[3]
    width, length = normed_t.shape
    half, quarter = length // 2, length // 4
    heads, blocks = biast.shape[:2]
    pairs = heads // 2
    inner = pairs * 128
    hidden = (grads.shape[4] - inner) // 3
    count = len(pieces)
    shape = jax.ShapeDtypeStruct
    vmem, hbm = pl.BlockSpec(memory_space=pltpu.VMEM), pl.BlockSpec(memory_space=pl.ANY)
    dma = pltpu.SemaphoreType.DMA
    lines = 2 * (width // 128) + buckets
    buffers = [piece_buffers(piece, deep, rows) for piece in pieces]
    scratch = [pltpu.VMEM(buffer[k], low) for k in range(4) for buffer in buffers]
    small = pltpu.VMEM((lines, 128), f32)
    scratch += [
        pltpu.VMEM((3 * pairs, length, 128), low),
        pltpu.VMEM((width, length), low),
        pltpu.VMEM((blocks, BAND * BLOCK, BLOCK), low),
        pltpu.VMEM((heads, blocks, BAND * BLOCK, BLOCK), low),
        pltpu.VMEM((deep, 2, 2, rows, 3 * inner), low),
        pltpu.VMEM((deep, 2, 2, rows, 128), low),
        pltpu.VMEM((pairs, length, 128), low),
        pltpu.VMEM((length, 256), f32),
        pltpu.VMEM((length, 256), low),
        pltpu.VMEM((2, heads, blocks, BLOCK), f32),
        pltpu.VMEM((length, 128), f32),
        pltpu.VMEM((length, 128), f32),
        pltpu.VMEM((length, 128), low),
        pltpu.VMEM((deep, 2, 2, rows, 3 * inner), low),
        pltpu.VMEM((2, quarter, width), f32),
        pltpu.VMEM((2, quarter, width), low),
        pltpu.VMEM((2, quarter, width), low),
        pltpu.VMEM((2, quarter, width), low),
        pltpu.VMEM((buckets * GROUP, heads * GROUP), f32),
        pltpu.VMEM((TURNS, buckets * GROUP, 2 * BLOCK), low),
        pltpu.VMEM((TURNS, heads * GROUP, 2 * BLOCK), low),
        small, small, small, small, small, pltpu.VMEM((deep, lines, 128), f32), small,
        dma((count,)),
        dma((count, 3, deep - 1)),
        dma((count, 3, deep - 1)),
        dma((12 + deep,)),
        dma((12 + deep,)),
        dma((9,)),
    ]
    return pl.pallas_call(
        functools.partial(back_kernel, shard_size, pieces, early, (inner, hidden, buckets)),
        out_shape=[
            shape((rows, 3 * hidden + inner), f32),
            shape((rows, 3 * inner), f32),
            shape((2, half, width), low),
            shape((2, half, width), low),
            shape((2, lines, 128), f32),
        ],
        in_specs=[pl.BlockSpec(memory_space=pltpu.SMEM)] + [hbm] * 7 + [vmem] * 6,
        out_specs=[vmem, vmem, hbm, hbm, vmem],
        scratch_shapes=scratch,
        compiler_params=pltpu.CompilerParams(
            collective_id=2, has_side_effects=True, vmem_limit_bytes=60 * MIB
        ),
        name="back",
    )(lengths, full, normed_t, qkv, bandt, biast, grads, do, lse, output, middle, tokens, gain_two, table_rows)


ORDERS = ("zyx", "zxy")
SUM_ORDERS = ("xyz", "yxz")
WINDOW = 6
ATTENTION_ACTS = 24


def shards(
    inputs, cotangent, lengths, buckets,
    query_weight, key_weight, value_weight, projection_weight, gate_weight, up_weight, down_weight,
    attention_gain, feedforward_gain, bias_table,
):
    x = lax.axis_index("ctx")
    shard_size = lax.axis_size("shard")
    width = inputs.shape[2]
    bucket_count, heads = bias_table.shape
    rows, inner = query_weight.shape
    hidden = gate_weight.shape[1]
    steps = hidden_steps(hidden)
    at_project = 128 + 3 * inner
    at_hidden = at_project + inner
    pieces = split_columns(0, at_project, 4) + split_columns(at_project, at_hidden, 2)
    for j, n in enumerate(steps):
        at = at_hidden + 3 * HIDDEN_STEP * j
        pieces += split_columns(at, at + 3 * n, 2)
    pieces = [(a, b, ORDERS[i % len(ORDERS)]) for i, (a, b) in enumerate(pieces)]

    gains = jnp.pad(jnp.stack([attention_gain, feedforward_gain], axis=1), ((0, 0), (0, 126)))
    table_rows = jnp.broadcast_to(
        jnp.pad(bias_table.astype(jnp.float32).T, ((0, 0), (0, 128 - bucket_count)))[:, None, :], (heads, 8, 128)
    )
    weights = (query_weight, key_weight, value_weight, projection_weight, gate_weight, up_weight, down_weight)
    (
        full, normed_t, qkv, bandt, biast, grads, grad_attended, tokens,
        lse, output, grad_middle, gain_two,
    ) = front(shard_size, pieces, WINDOW, lengths, gains, weights, inputs, cotangent, buckets, table_rows)

    cuts = [(0, a, b) for a, b in split_columns(0, 3 * hidden + inner, 12)]
    early = len(cuts)
    cuts += [(1, a, b) for t in range(3) for a, b in split_columns(t * inner, (t + 1) * inner, 1)]
    cuts = [(t, a, b, SUM_ORDERS[i % len(SUM_ORDERS)]) for i, (t, a, b) in enumerate(cuts)]
    gain_two = jnp.sum(gain_two, axis=(0, 1)).reshape(-1, 128)
    hidden_sums, weight_sums, output, input_grad, small = back(
        shard_size, cuts, early, bucket_count,
        lengths, full, normed_t, qkv, bandt, biast, grads, grad_attended,
        lse, output, grad_middle, tokens, gain_two, table_rows,
    )
    at = [3 * HIDDEN_STEP * j for j in range(len(steps))]
    gate, up, down = [
        jnp.concatenate([hidden_sums[:, a + k * n : a + (k + 1) * n] for a, n in zip(at, steps)], axis=1) for k in range(3)
    ]
    lines = width // 128
    me = lax.axis_index("shard") * 2 + x

    def own_gain(part):
        return lax.dynamic_slice_in_dim(small[1, part * lines : (part + 1) * lines].reshape(-1), me * rows, rows)

    return (
        output, input_grad.astype(jnp.float32),
        weight_sums[:, :inner], weight_sums[:, inner : 2 * inner], weight_sums[:, 2 * inner :], hidden_sums[:, 3 * hidden :],
        gate, up, down, own_gain(0), own_gain(1), small[0, 2 * lines :, :heads],
    )


def solution(mesh):
    rows = P(None, ("shard", "ctx"), None)
    weight = P(("shard", "ctx"), "tp")
    gain = P(("shard", "ctx"))
    table = P(None, "tp")
    return jax.shard_map(
        shards,
        mesh=mesh,
        in_specs=(rows, rows, P(None, "shard"), P("ctx", None)) + (weight,) * 7 + (gain, gain, table),
        out_specs=(rows, rows) + (weight,) * 7 + (gain, gain, table),
        check_vma=False,
    )
```

profile of v0, /device:TPU:0, one launch (start us, length us, event | category | flops | bytes accessed | tf_op | source)
XLA Modules:
  0.0 435.8 jit_solution(10741754475277686051)
XLA Ops:
  0.6 0.7 pad_convert_fusion
  1.3 0.6 broadcast_in_dim.2.table_ref.refs_13_
  1.9 1.3 copy.33.lengths_ref.refs_0_
  3.2 0.7 pad_maximum_fusion
  3.9 0.1 copy.31
  4.0 0.6 pad.11.gains_ref
  4.7 192.1 %front.1 = (bf16[4,2,2,64,6400]{4,3,2,1,0:T(8,128)(2,1)}, bf16[1024,1024]{1,0:T(8,128)(2,1)}, bf16[12,1024,128]{2,1,0:T(8,128)(2,1)}, bf16[8,384,128]{2,1,0:T(8,...) custom-call(s32[2,1]{1,0:T(2,128)} %copy.33.lengths_ref.refs_0_, ...), custom_call_target="tpu_custom_call" | custom-call | tf_op jit(solution)/shard_map/front/pallas_call | solution.py:699
  196.7 1.4 reduce_sum.9
  198.2 223.9 %back.1 = (f32[64,4736]{1,0:T(8,128)}, f32[64,1536]{1,0:T(8,128)}, bf16[2,512,1024]{2,1,0:T(8,128)(2,1)}, bf16[2,512,1024]{2,1,0:T(8,128)(2,1)}, f32[2,48,128]{2,1,0:T(8,128)}) custom-call(s32[2,1]{1,0:T(2,128)} %copy.33.lengths_ref.refs_0_, bf16[4,2,2,64,6400]{4,3,2,1,0:T(8,128)(2,1)} %get-tuple-element.29.refs_1_, ...), custom_call_target="tpu_custom_call" | custom-call | tf_op jit(solution)/shard_map/back/pallas_call | solution.py:1212
  422.0 0.0 copy-start
  422.1 1.1 slice_dynamic-update-slice_fusion.4
  423.1 0.9 slice_dynamic-update-slice_fusion.3
  424.1 0.9 slice_dynamic-update-slice_fusion.2
  425.0 0.9 slice_dynamic-update-slice_fusion.1
  425.9 0.9 slice_dynamic-update-slice_fusion
  426.8 0.8 constant_dynamic-update-slice_fusion.2
  427.6 0.0 copy-start.4
  427.6 0.0 copy-start.5
  427.6 0.0 copy-start.6
  427.7 0.0 copy-done
  427.7 0.0 copy-start.2
  427.7 0.0 copy-start.3
  427.7 0.0 copy-start.1
  427.7 2.6 convert_element_type.8
  430.3 0.0 copy-done.4
  430.3 0.0 copy-done.5
  430.3 0.0 copy-done.6
  430.3 0.0 copy-done.2
  430.3 0.8 fusion
  431.1 1.6 slice.78
  432.6 0.0 copy-done.3
  432.6 0.6 dynamic_slice.6
  433.2 0.6 dynamic_slice.7
  433.8 0.7 copy.34
  434.5 0.0 copy-done.1
  434.5 1.3 copy.51
  (2 shorter events, 0.0 us)
Async XLA Ops:
  422.0 5.6 %copy-start = (bf16[2,512,1024]{2,1,0:T(8,128)(2,1)S(1)}, bf16[2,512,1024]{2,1,0:T(8,128)(2,1)}, u32[]{:S(2)}) copy-start(bf16[2,512,1024]{2,1,0:T(8,128)(2,1)} %get-tuple-element.42) | copy-start | bytes 6291460
  427.6 2.7 copy-start.4
  427.6 2.7 copy-start.5
  427.6 2.7 copy-start.6
  427.7 2.6 copy-start.2
  427.7 5.0 %copy-start.3 = (f32[2,48,128]{2,1,0:T(8,128)S(1)}, f32[2,48,128]{2,1,0:T(8,128)}, u32[]{:S(2)}) copy-start(f32[2,48,128]{2,1,0:T(8,128)} %get-tuple-element.45) | copy-start | bytes 147460
  427.7 6.8 %copy-start.1 = (bf16[2,512,1024]{2,1,0:T(8,128)(2,1)S(1)}, bf16[2,512,1024]{2,1,0:T(8,128)(2,1)}, u32[]{:S(2)}) copy-start(bf16[2,512,1024]{2,1,0:T(8,128)(2,1)} %get-tuple-element.105) | copy-start | bytes 6291460
where the time goes:
time: 436 us
  Pallas kernels  416 us (95%)
  local copies, waits for them, and re-layouts  13.7 us (3%)
  other arithmetic  5.41 us (1%)
    pallas_call x1, Pallas kernels, back(): pl.pallas_call(functools.partial(back_kernel, shard_size, pieces, early,...  224 us
    pallas_call x1, Pallas kernels, front(): pl.pallas_call(functools.partial(front_kernel, shard_size, pieces, window...  192 us

commit v1 on v0

--- a/solution.py
+++ b/solution.py
@@ -143,11 +143,13 @@
                 self.start(piece, 2)
             return act
 
-        for piece in range(count + 1):
+        turned = 0
+        for piece in range(count + LAG):
             if piece < count:
                 self.queue.append((None, second(piece)))
-            if piece > 0:
-                self.queue.append((piece - 1, third(piece - 1)))
+            while turned < count and turned <= piece - (1 if turned < QUICK else LAG):
+                self.queue.append((turned, third(turned)))
+                turned += 1
         for piece in range(min(window, count)):
             self.start(piece, 0)
 
@@ -163,6 +165,7 @@
         for piece in pieces:
             while any(mark == piece for mark, _ in self.queue):
                 self.run(1)
+        self.run(AHEAD)
         for piece in pieces:
             self.arrive(piece, 2)
 
@@ -181,6 +184,14 @@
     return jnp.concatenate(parts, axis=0).astype(jnp.bfloat16)
 
 
+def between(acts, units, skip, unit, head):
+    slots = 2 * units - skip
+    for k, act in enumerate(acts):
+        slot = skip + (k * slots) // len(acts)
+        if slot % 2 == head:
+            pl.when(unit == slot // 2)(act)
+
+
 def gelu_all(gate):
     square = gate * gate
     tangent = jnp.tanh(GELU_ROOT * (gate + GELU_CUBIC * square * gate))
@@ -197,7 +208,7 @@
     inputs_ref, cots_ref, buckets_ref, table_ref,
     full_ref, normed_out, qkv_out, bandt_out, biast_out, grads_out, attended_out, tokens_own_ref,
     lse_ref, output_ref, middle_grad_ref, gain_ref,
-    own_ref, tok, cot, band, bandt, bias, biast, kaux, gain_buf, qkv, normed, scores, attended, project_w,
+    own_ref, tok, cot, band_raw, band, bandt, bias, biast, kaux, gain_buf, qkv, normed, scores, attended, project_w,
     normal, away, arrived, two_t, low_t, acc_out, acc_two, w_buf, g_buf, hid, ggate, gup,
     send_sem, recv_sem, near_send, near_recv, local_sem, w_sem, g_sem, own_sem, bt_sem,
 ):
@@ -246,7 +257,7 @@
     own_tok = own_load(0, inputs_ref.at[x], tok.at[pl.ds(x * half, half)])
     own_cot = own_load(1, cots_ref.at[x], cot.at[pl.ds(x * half, half)])
     own_bands = [
-        own_load(13 + i, band_source(x * (blocks // 2) + i), band.at[x * (blocks // 2) + i]) for i in range(blocks // 2)
+        own_load(13 + i, band_source(x * (blocks // 2) + i), band_raw.at[i]) for i in range(blocks // 2)
     ]
     own_full = own_load(3, own_ref, full_ref.at[place.z, place.y, x])
     for copy in (*own_loads, *own_bands, own_tok, own_cot):
@@ -267,37 +278,39 @@
 
     mine = [x * (blocks // 2) + c * (blocks // 4) + i for i in range(blocks // 4)]
     theirs = [(1 - x) * (blocks // 2) + c * (blocks // 4) + i for i in range(blocks // 4)]
-    band_x = [near(16 + i, band_source(block), band.at[block], to_x) for i, block in enumerate(mine)]
+    band_x = [near(16 + i, band.at[block], band.at[block], to_x) for i, block in enumerate(mine)]
     tok_x = near(1, inputs_ref.at[1 - x, pl.ds(c * quarter, quarter)], tok.at[x_rows(x, c)], to_x)
     cot_x = near(2, cots_ref.at[1 - x, pl.ds(c * quarter, quarter)], cot.at[x_rows(x, c)], to_x)
     band_c = [near(16 + len(mine) + i, band.at[block], band.at[block], to_c) for i, block in enumerate(theirs)]
     tok_c = near(4, tok.at[x_rows(1 - x, c)], tok.at[x_rows(1 - x, c)], to_c)
     cot_c = near(5, cot.at[x_rows(1 - x, c)], cot.at[x_rows(1 - x, c)], to_c)
+    gather.plan(window)
+    for copy in own_bands:
+        copy.wait()
+    for i in range(blocks // 2):
+        band[x * (blocks // 2) + i] = band_raw[i].astype(jnp.float32).astype(low)
     for copy in band_x:
         copy.start()
     tok_x.start()
-    gather.plan(window)
-    cot_x.start()
     own_full.wait()
     lanes_of = lax.broadcasted_iota(jnp.int32, (length, 128), 1)
     rows_of = lax.broadcasted_iota(jnp.int32, (length, 128), 0)
     valid = lengths_ref[x, 0]
     blocked = jnp.where(rows_of // BLOCK == lanes_of, 1.0, 0.0)
     kaux[...] = jnp.where((lanes_of == blocks) & (rows_of >= valid), -1e30, blocked).astype(low)
+    gather.run(1)
     for copy in band_x:
         copy.wait()
     for copy in band_c:
         copy.start()
-    tok_x.wait()
-    tok_c.start()
-    for copy in (*own_bands, *band_c):
+    gather.run(1)
+    for copy in band_c:
         copy.wait()
-    gather.run(2)
 
     def bias_step(i, carry):
         block = i // (BLOCK // 16)
         at = pl.multiple_of((i % (BLOCK // 16)) * 16, 16)
-        index = band[block, pl.ds(at, 16), :]
+        index = band[block, pl.ds(at, 16), :].astype(jnp.float32).astype(jnp.int32)
         for col in range(BAND):
             lanes = slice(col * BLOCK, (col + 1) * BLOCK)
             for head in range(heads):
@@ -306,10 +319,13 @@
                 bias[head, block, pl.ds(at, 16), lanes] = jnp.concatenate(got, axis=0).astype(low)
         return carry
 
-    lax.fori_loop(0, blocks * (BLOCK // 16) // 2, bias_step, 0)
-    gather.run(4)
-    lax.fori_loop(blocks * (BLOCK // 16) // 2, blocks * (BLOCK // 16), bias_step, 0)
-    gather.run(2)
+    bias_steps = blocks * (BLOCK // 16)
+    for k in range(4):
+        lax.fori_loop(bias_steps * k // 4, bias_steps * (k + 1) // 4, bias_step, 0)
+        gather.run(1)
+    tok_x.wait()
+    tok_c.start()
+    cot_x.start()
 
     def biast_store(block, slot):
         return pltpu.make_async_copy(biast.at[slot], biast_out.at[:, block], bt_sem.at[slot])
@@ -335,20 +351,15 @@
         biast_store(block, slot).start()
         return carry
 
-    lax.fori_loop(0, blocks // 2, biast_block, 0)
-    gather.run(4)
-    lax.fori_loop(blocks // 2, blocks, biast_block, 0)
-    gather.run(2)
+    for k in range(4):
+        lax.fori_loop(blocks * k // 4, blocks * (k + 1) // 4, biast_block, 0)
+        gather.run(1)
     biast_store(blocks - 2, 0).wait()
     biast_store(blocks - 1, 1).wait()
     bandt_store = own_load(4, bandt, bandt_out)
     bandt_store.start()
     own_tok.wait()
     tok_c.wait()
-    own_cot.wait()
-    cot_x.wait()
-    cot_c.start()
-    cot_c.wait()
 
     def live_step(i, carry):
         rows = pl.ds(pl.multiple_of(i * BLOCK, BLOCK), BLOCK)
@@ -357,8 +368,6 @@
         cot[rows, :] = masked
         low_t[:, rows] = jnp.transpose(masked)
         return carry
-
-    lax.fori_loop(0, blocks, live_step, 0)
 
     gather.need(qkv_pieces)
     load_gains = own_load(5, full_ref.at[:, :, :, :, 0:at_q], gain_buf)
@@ -411,13 +420,9 @@
     qkv_store.start()
 
     units = pairs * (length // 256)
-    acts = gather.take(min(len(gather.queue), 10))
+    acts = gather.take(min(len(gather.queue), FORWARD_ACTS))
 
     def unit_step(unit, carry):
-        for k, act in enumerate(acts):
-            @pl.when(unit == (k * units) // len(acts))
-            def _(act=act):
-                act()
         pair = unit // (length // 256)
         step = unit % (length // 256)
         rows = pl.ds(pl.multiple_of(step * 256, 256), 256)
@@ -425,6 +430,7 @@
         keys = jnp.concatenate([qkv[pairs + pair], kaux[...]], axis=1)
         outs = []
         for head in range(2):
+            between(acts, units, 0, unit, head)
             aux = query_aux(table_ref[2 * pair + head], step, blocks)
             masked = jnp.where(lane_head(256, 128, head), queries, jnp.zeros_like(queries))
             scores[...] = lax.dot_general(
@@ -448,6 +454,10 @@
         return carry
 
     lax.fori_loop(0, units, unit_step, 0)
+    own_cot.wait()
+    cot_x.wait()
+    cot_c.start()
+
     normed_store.wait()
     two = normed
     gather.need(project_pieces)
@@ -484,7 +494,7 @@
         inverse = lax.rsqrt(jnp.mean(middle * middle, axis=-1, keepdims=True) + EPSILON)
         two[part_rows(part, c), :] = (middle * inverse * gain_two).astype(low)
         share(8, part, two).start()
-    gather.run(2)
+    gather.run(1)
     for part in range(2):
         share(8, part, two).wait()
 
@@ -494,7 +504,10 @@
         return carry
 
     lax.fori_loop(0, blocks, turn_step, 0)
-    gather.run(2)
+    gather.run(1)
+    cot_c.wait()
+    lax.fori_loop(0, blocks, live_step, 0)
+    gather.run(1)
 
     def bounds(j):
         at = at_hidden + 3 * HIDDEN_STEP * j
@@ -546,7 +559,7 @@
             return carry
 
         lax.fori_loop(0, length // 256, rows_step, 0)
-        gather.run(2)
+        gather.run(1)
         if j + 1 < len(steps):
             first = first_hidden_piece + per_step * (j + 1)
             gather.need(range(first, first + per_step))
@@ -663,7 +676,8 @@
         pltpu.VMEM((rows, wide), low),
         pltpu.VMEM((length, width), low),
         pltpu.VMEM((length, width), low),
-        pltpu.VMEM((blocks, BLOCK, BAND * BLOCK), jnp.int32),
+        pltpu.VMEM((blocks // 2, BLOCK, BAND * BLOCK), jnp.int32),
+        pltpu.VMEM((blocks, BLOCK, BAND * BLOCK), low),
         pltpu.VMEM((blocks, BAND * BLOCK, BLOCK), low),
         pltpu.VMEM((heads, blocks, BLOCK, BAND * BLOCK), low),
         pltpu.VMEM((2, heads, BAND * BLOCK, BLOCK), low),
@@ -729,9 +743,11 @@
         return [name for name in "zyx" if name != order[0]]
 
     def cut(self, piece, name, value):
-        t, a, b, _ = self.pieces[piece]
+        t, a, b = self.pieces[piece][:3]
         at = [value if name == other else slice(None) for other in "zyx"]
-        return self.sources[t].at[at[0], at[1], at[2], :, a:b]
+        if t:
+            return self.sources[1].at[t - 1, at[0], at[1], at[2]]
+        return self.sources[0].at[at[0], at[1], at[2], :, a:b]
 
     def own_copy(self, piece):
         order = self.pieces[piece][3]
@@ -777,15 +793,16 @@
         for copy in self.copies(piece, hop):
             copy.wait_recv()
 
-    def begin(self, pieces):
-        for piece in pieces:
-            self.start(piece, 0)
-            self.own_copy(piece).start()
+    def begin(self, piece):
+        self.start(piece, 0)
+        self.own_copy(piece).start()
 
     def add_first(self, piece):
         order = self.pieces[piece][3]
         self.arrive(piece, 0)
         self.own_copy(piece).wait()
+        if piece + self.window < self.early:
+            self.begin(piece + self.window)
         own, came = self.own[piece], self.first[piece]
         inner = own.shape[1]
 
@@ -812,7 +829,12 @@
         spans = own.shape[1] if rest[0] == name else own.shape[0]
 
         def body(i, carry):
-            if rest[0] == name:
+            if name == "z":
+                total = own[mine, i].astype(jnp.float32)
+                for d in range(came.shape[0]):
+                    total = total + came[d, i].astype(jnp.float32)
+                own[mine, i] = total.astype(jnp.bfloat16)
+            elif rest[0] == name:
                 own[mine, i] = own[mine, i] + came[i]
             else:
                 own[i, mine] = own[i, mine] + came[i]
@@ -823,7 +845,6 @@
 
     def add_third(self, piece):
         place, order = self.place, self.pieces[piece][3]
-        t, a, b, _ = self.pieces[piece]
         rest = self.rest(piece)
         self.arrive(piece, 2)
         total = self.own[piece][getattr(place, rest[0]), getattr(place, rest[1])].astype(jnp.float32)
@@ -832,17 +853,21 @@
                 total = total + self.third[piece][d - 1].astype(jnp.float32)
         else:
             total = total + self.third[piece][...].astype(jnp.float32)
-        self.outs[t][:, a:b] = total
-
-    def plan(self, pieces):
-        pieces = list(pieces)
-        for i in range(len(pieces) + 2):
-            if i < len(pieces):
-                self.queue.append(functools.partial(self.add_first, pieces[i]))
-            if 0 < i <= len(pieces):
-                self.queue.append(functools.partial(self.add_second, pieces[i - 1]))
-            if i > 1:
-                self.queue.append(functools.partial(self.add_third, pieces[i - 2]))
+        for out, start, at, n in self.pieces[piece][4]:
+            self.outs[out][:, start : start + n] = total[:, at : at + n]
+
+    def plan(self, window, early):
+        self.window, self.early = window, early
+        count = len(self.pieces)
+        for i in range(count + SUM_LAGS[1]):
+            if i < count:
+                self.queue.append(functools.partial(self.add_first, i))
+            if 0 <= i - SUM_LAGS[0] < count:
+                self.queue.append(functools.partial(self.add_second, i - SUM_LAGS[0]))
+            if 0 <= i - SUM_LAGS[1] < count:
+                self.queue.append(functools.partial(self.add_third, i - SUM_LAGS[1]))
+        for i in range(min(window, early)):
+            self.begin(i)
 
     def run(self, steps):
         for _ in range(min(steps, len(self.queue))):
@@ -860,7 +885,7 @@
 
 
 def piece_buffers(piece, deep, rows):
-    _, a, b, order = piece
+    _, a, b, order, _ = piece
     sizes = {"z": deep, "y": 2, "x": 2}
     rest = [name for name in "zyx" if name != order[0]]
     left = [sizes[name] for name in rest]
@@ -881,8 +906,8 @@
         lse_ref, output_ref, middle_ref, tokens_ref, gain_two_ref, table_ref,
     ) = refs[:14]
     refs = refs[14:]
-    hidden_out, weight_sums, output_out, input_out, small_out = refs[:5]
-    refs = refs[5:]
+    weight_outs, (output_out, input_out, small_out) = refs[:7], refs[7:10]
+    refs = refs[10:]
     first, own, second, third = [refs[k * count : (k + 1) * count] for k in range(4)]
     refs = refs[4 * count :]
     (
@@ -914,10 +939,9 @@
         copy.start()
     meet(place)
     scatter = Scatter(
-        place, pieces, (grads_in, wgrad), (hidden_out, weight_sums), (first, own, second, third), (own_sem, send_sem, recv_sem),
+        place, pieces, (grads_in, wgrad), weight_outs, (first, own, second, third), (own_sem, send_sem, recv_sem),
     )
-    scatter.begin(range(early))
-    scatter.plan(range(early))
+    scatter.plan(SUM_WINDOW, early)
 
     def near(i, source, target, device):
         return send(source, target, near_send.at[i], near_recv.at[i], device)
@@ -942,7 +966,7 @@
     blocked = jnp.where(rows_of // BLOCK == lanes_of, 1.0, 0.0)
     kaux[...] = jnp.where((lanes_of == blocks) & (rows_of >= valid), -1e30, blocked).astype(low)
     far[...] = jnp.zeros_like(far)
-    for copy in loads[:3]:
+    for copy in loads:
         copy.wait()
 
     per_pair = length // 256
@@ -950,10 +974,6 @@
     acts = scatter.take(ATTENTION_ACTS)
 
     def unit_step(unit, carry):
-        for k, act in enumerate(acts):
-            @pl.when(unit == (k * units) // len(acts))
-            def _(act=act):
-                act()
         pair = unit // per_pair
         step = unit % per_pair
         rows = pl.ds(pl.multiple_of(step * 256, 256), 256)
@@ -970,6 +990,7 @@
         values = qkv[2 * pairs + pair]
         dq = None
         for head in range(2):
+            between(acts, units, ACT_FIRST, unit, head)
             here = lane_head(256, 128, head)
             aux = query_aux(table_ref[2 * pair + head], step, blocks)
             q_masked = jnp.where(here, queries, jnp.zeros_like(queries))
@@ -1013,6 +1034,21 @@
         def _():
             qkv[pairs + pair] = dk_acc[...].astype(low)
             qkv[2 * pairs + pair] = dv_acc[...].astype(low)
+            right = jnp.concatenate([qkv[t * pairs + pair] for t in range(3)], axis=1)
+
+            def weight_step(i, carry):
+                rows = pl.ds(pl.multiple_of(i * 256, 256), 256)
+                got = jnp.dot(normed_t[rows, :], right, preferred_element_type=f32).astype(low)
+                span = deep // (width // 256)
+                wgrad[pair, pl.ds(i * span, span)] = got.reshape((span,) + wgrad.shape[2:5] + (3 * 128,))
+                return carry
+
+            lax.fori_loop(0, width // 256, weight_step, 0)
+
+        for late in range(early, count):
+            @pl.when(unit == (late - early + 1) * per_pair - 1)
+            def _(late=late):
+                scatter.begin(late)
 
         return carry
 
@@ -1020,26 +1056,6 @@
     for copy in output_moves[:3]:
         copy.wait()
     output_moves[3].start()
-    for copy in loads[3:]:
-        copy.wait()
-
-    for t in range(3):
-        def weight_step(i, carry, t=t):
-            rows = pl.ds(pl.multiple_of(i * 256, 256), 256)
-            right = jnp.concatenate([qkv[t * pairs + pair] for pair in range(pairs)], axis=1)
-            got = jnp.dot(normed_t[rows, :], right, preferred_element_type=f32).astype(low)
-            span = deep // (width // 256)
-            wgrad[pl.ds(i * span, span), :, :, :, t * inner : (t + 1) * inner] = got.reshape(
-                (span,) + wgrad.shape[1:4] + (inner,)
-            )
-            return carry
-
-        lax.fori_loop(0, width // 256, weight_step, 0)
-        late = [i for i in range(early, count) if t * inner <= pieces[i][1] < (t + 1) * inner]
-        scatter.begin(late)
-        scatter.plan(late)
-        scatter.run(2)
-
     def part_rows(part, core):
         return pl.ds(pl.multiple_of(part * half + core * quarter, quarter), quarter)
 
@@ -1060,7 +1076,9 @@
     lax.fori_loop(0, 2, away_step, 0)
     for copy in swaps:
         copy.start()
+    scatter.run(1)
     lax.fori_loop(0, 2, mine_step, 0)
+    scatter.run(1)
     gains = jnp.transpose(gain_buf[...].reshape(width, 128).astype(f32))
     gain_one = gains[0:1, :]
     gain_sum = jnp.zeros((1, width), f32)
@@ -1074,15 +1092,14 @@
         scaled = total * gain_one
         back = inverse * (scaled - unit * jnp.mean(scaled * unit, axis=-1, keepdims=True))
         result[part] = (middle_ref[part] + back).astype(low)
+        scatter.run(1)
     input_moves = to_owners(1, result, input_out)
     for copy in input_moves[:3]:
         copy.start()
-    scatter.run(2)
-
     table_acc[...] = jnp.zeros_like(table_acc)
     groups = BAND * BLOCK // GROUP
     table_units = blocks // 2 * groups // TURNS
-    table_acts = scatter.take(len(scatter.queue))
+    table_acts = scatter.take(TABLE_ACTS)
 
     def table_step(i, carry):
         for k, act in enumerate(table_acts):
@@ -1135,19 +1152,23 @@
 
     move = near(small_base, small, small_x, to_x)
     move.start()
+    scatter.run(1)
     move.wait()
     hold_x[...] = small[...] + small_x[...]
     move = near(small_base + 1, hold_x, small_y, to_y)
     move.start()
+    scatter.run(1)
     move.wait()
     hold_z[z] = hold_x[...] + small_y[...]
     for d in range(1, deep):
         small_line(d).start()
+    scatter.run(1)
     for d in range(1, deep):
         small_line(d).wait()
     hold_y[...] = jnp.sum(hold_z[...], axis=0)
     move = near(small_base + 2, hold_y, small_c, to_c)
     move.start()
+    scatter.run(1)
     move.wait()
     small_out[0] = hold_y[...]
     small_out[1] = hold_y[...] + small_c[...]
@@ -1193,7 +1214,7 @@
         pltpu.VMEM((length, 128), f32),
         pltpu.VMEM((length, 128), f32),
         pltpu.VMEM((length, 128), low),
-        pltpu.VMEM((deep, 2, 2, rows, 3 * inner), low),
+        pltpu.VMEM((pairs, deep, 2, 2, rows, 3 * 128), low),
         pltpu.VMEM((2, quarter, width), f32),
         pltpu.VMEM((2, quarter, width), low),
         pltpu.VMEM((2, quarter, width), low),
@@ -1212,14 +1233,13 @@
     return pl.pallas_call(
         functools.partial(back_kernel, shard_size, pieces, early, (inner, hidden, buckets)),
         out_shape=[
-            shape((rows, 3 * hidden + inner), f32),
-            shape((rows, 3 * inner), f32),
+            *[shape((rows, n), f32) for n in (inner,) * 4 + (hidden,) * 3],
             shape((2, half, width), low),
             shape((2, half, width), low),
             shape((2, lines, 128), f32),
         ],
         in_specs=[pl.BlockSpec(memory_space=pltpu.SMEM)] + [hbm] * 7 + [vmem] * 6,
-        out_specs=[vmem, vmem, hbm, hbm, vmem],
+        out_specs=[vmem] * 7 + [hbm, hbm, vmem],
         scratch_shapes=scratch,
         compiler_params=pltpu.CompilerParams(
             collective_id=2, has_side_effects=True, vmem_limit_bytes=60 * MIB
@@ -1228,10 +1248,53 @@
     )(lengths, full, normed_t, qkv, bandt, biast, grads, do, lse, output, middle, tokens, gain_two, table_rows)
 
 
-ORDERS = ("zyx", "zxy")
-SUM_ORDERS = ("xyz", "yxz")
-WINDOW = 6
-ATTENTION_ACTS = 24
+ORDERS = ("xyz", "zxy", "zyx", "zxy", "zxy", "zyx", "zxy", "zyx", "zxy")
+SUM_ORDERS = ("yxz", "xyz", "yzx", "yxz", "xzy", "yxz")
+WINDOW = 4
+AHEAD = 4
+LAG = 3
+QUICK = 4
+SUM_WINDOW = 3
+SUM_LAGS = (2, 4)
+FORWARD_ACTS = 8
+ATTENTION_ACTS = 20
+ACT_FIRST = 5
+TABLE_ACTS = 7
+
+
+def front_pieces(inner, hidden):
+    at_project = 128 + 3 * inner
+    at_hidden = at_project + inner
+    pieces = split_columns(0, at_project, 4) + split_columns(at_project, at_hidden, 2)
+    for j, n in enumerate(hidden_steps(hidden)):
+        at = at_hidden + 3 * HIDDEN_STEP * j
+        pieces += split_columns(at, at + 3 * n, 2)
+    return [(a, b, ORDERS[i % len(ORDERS)]) for i, (a, b) in enumerate(pieces)]
+
+
+def back_pieces(inner, hidden):
+    where = []
+    for j, n in enumerate(hidden_steps(hidden)):
+        for k in range(3):
+            where.append((3 * HIDDEN_STEP * j + k * n, n, 4 + k, HIDDEN_STEP * j))
+    where.append((3 * hidden, inner, 3, 0))
+    cuts = []
+    for j, n in enumerate(hidden_steps(hidden)):
+        at = 3 * HIDDEN_STEP * j
+        cuts += split_columns(at, at + 3 * n, 2 if n > 128 else 1)
+    cuts += split_columns(3 * hidden, 3 * hidden + inner, 2)
+    pieces = []
+    for a, b in cuts:
+        segments = []
+        for start, n, out, column in where:
+            low, high = max(a, start), min(b, start + n)
+            if low < high:
+                segments.append((out, column + low - start, low - a, high - low))
+        pieces.append((0, a, b, segments))
+    early = len(pieces)
+    for pair in range(inner // 128):
+        pieces.append((1 + pair, 0, 3 * 128, [(t, pair * 128, t * 128, 128) for t in range(3)]))
+    return [(t, a, b, SUM_ORDERS[i % len(SUM_ORDERS)], segments) for i, (t, a, b, segments) in enumerate(pieces)], early
 
 
 def shards(
@@ -1245,15 +1308,6 @@
     bucket_count, heads = bias_table.shape
     rows, inner = query_weight.shape
     hidden = gate_weight.shape[1]
-    steps = hidden_steps(hidden)
-    at_project = 128 + 3 * inner
-    at_hidden = at_project + inner
-    pieces = split_columns(0, at_project, 4) + split_columns(at_project, at_hidden, 2)
-    for j, n in enumerate(steps):
-        at = at_hidden + 3 * HIDDEN_STEP * j
-        pieces += split_columns(at, at + 3 * n, 2)
-    pieces = [(a, b, ORDERS[i % len(ORDERS)]) for i, (a, b) in enumerate(pieces)]
-
     gains = jnp.pad(jnp.stack([attention_gain, feedforward_gain], axis=1), ((0, 0), (0, 126)))
     table_rows = jnp.broadcast_to(
         jnp.pad(bias_table.astype(jnp.float32).T, ((0, 0), (0, 128 - bucket_count)))[:, None, :], (heads, 8, 128)
@@ -1262,22 +1316,15 @@
     (
         full, normed_t, qkv, bandt, biast, grads, grad_attended, tokens,
         lse, output, grad_middle, gain_two,
-    ) = front(shard_size, pieces, WINDOW, lengths, gains, weights, inputs, cotangent, buckets, table_rows)
-
-    cuts = [(0, a, b) for a, b in split_columns(0, 3 * hidden + inner, 12)]
-    early = len(cuts)
-    cuts += [(1, a, b) for t in range(3) for a, b in split_columns(t * inner, (t + 1) * inner, 1)]
-    cuts = [(t, a, b, SUM_ORDERS[i % len(SUM_ORDERS)]) for i, (t, a, b) in enumerate(cuts)]
+    ) = front(shard_size, front_pieces(inner, hidden), WINDOW, lengths, gains, weights, inputs, cotangent, buckets, table_rows)
+
+    cuts, early = back_pieces(inner, hidden)
     gain_two = jnp.sum(gain_two, axis=(0, 1)).reshape(-1, 128)
-    hidden_sums, weight_sums, output, input_grad, small = back(
+    *weight_sums, output, input_grad, small = back(
         shard_size, cuts, early, bucket_count,
         lengths, full, normed_t, qkv, bandt, biast, grads, grad_attended,
         lse, output, grad_middle, tokens, gain_two, table_rows,
     )
-    at = [3 * HIDDEN_STEP * j for j in range(len(steps))]
-    gate, up, down = [
-        jnp.concatenate([hidden_sums[:, a + k * n : a + (k + 1) * n] for a, n in zip(at, steps)], axis=1) for k in range(3)
-    ]
     lines = width // 128
     me = lax.axis_index("shard") * 2 + x
 
@@ -1286,8 +1333,7 @@
 
     return (
         output, input_grad.astype(jnp.float32),
-        weight_sums[:, :inner], weight_sums[:, inner : 2 * inner], weight_sums[:, 2 * inner :], hidden_sums[:, 3 * hidden :],
-        gate, up, down, own_gain(0), own_gain(1), small[0, 2 * lines :, :heads],
+        *weight_sums, own_gain(0), own_gain(1), small[0, 2 * lines :, :heads],
     )
 
 

time: 436 us -> 360 us (0.83)
  Pallas kernels: 416 us -> 341 us
    pallas_call x1, Pallas kernels: 224 us -> 163 us  [back(): pl.pallas_call(functools.partial(back_kernel, shard_size, pieces, early,...]
    pallas_call x1, Pallas kernels: 192 us -> 178 us  [front(): pl.pallas_call(functools.partial(front_kernel, shard_size, pieces, window...]
where the time goes in v1:
time: 360 us; the launch traced here: 359 us
  Pallas kernels  341 us (95%)
  local copies, waits for them, and re-layouts  10.7 us (3%)
  other arithmetic  7.03 us (2%)
    pallas_call x1, Pallas kernels, front(): pl.pallas_call(functools.partial(front_kernel, shard_size, pieces, window...  178 us
    pallas_call x1, Pallas kernels, back(): pl.pallas_call(functools.partial(back_kernel, shard_size, pieces, early,...  163 us
    unnamed x28, local copies, waits for them, and re-layouts  8.14 us

profile of v1, /device:TPU:0, one launch (start us, length us, event | category | flops | bytes accessed | tf_op | source)
XLA Modules:
  0.0 359.4 jit_solution(12685588338680757016)
XLA Ops:
  0.6 0.7 pad_convert_fusion
  1.3 0.6 broadcast_in_dim.2.table_ref.refs_13_
  1.9 1.3 copy.33.lengths_ref.refs_0_
  3.2 0.7 pad_maximum_fusion
  3.9 0.1 copy.31
  4.0 0.6 pad.11.gains_ref
  4.7 178.0 %front.1 = (bf16[4,2,2,64,6400]{4,3,2,1,0:T(8,128)(2,1)}, bf16[1024,1024]{1,0:T(8,128)(2,1)}, bf16[12,1024,128]{2,1,0:T(8,128)(2,1)}, bf16[8,384,128]{2,1,0:T(8,...) custom-call(s32[2,1]{1,0:T(2,128)} %copy.33.lengths_ref.refs_0_, ...), custom_call_target="tpu_custom_call" | custom-call | tf_op jit(solution)/shard_map/front/pallas_call | solution.py:713
  182.6 1.4 reduce_sum.9
  184.1 163.0 %back.1 = (f32[64,512]{1,0:T(8,128)}, f32[64,512]{1,0:T(8,128)}, f32[64,512]{1,0:T(8,128)}, f32[64,512]{1,0:T(8,128)}, f32[64,1408]{1,0:T(8,128)}, /*index=5*/f3...) custom-call(s32[2,1]{1,0:T(2,128)} %copy.33.lengths_ref.refs_0_, ...), custom_call_target="tpu_custom_call" | custom-call | tf_op jit(solution)/shard_map/back/pallas_call | solution.py:1233
  347.1 0.0 copy-start.8
  347.1 0.0 copy-start
  347.1 4.2 %convert_element_type.8 = f32[2,512,1024]{2,1,0:T(8,128)} convert(bf16[2,512,1024]{2,1,0:T(8,128)(2,1)} %get-tuple-element.47) | non-fusion elementwise | flops 1048576 | bytes 6291456 | tf_op jit(solution)/shard_map/convert_element_type | solution.py:1335
  351.3 0.0 copy-done.8
  351.3 0.6 dynamic_slice.6
  351.9 0.6 dynamic_slice.7
  352.5 0.7 copy.34
  353.1 0.0 copy-done
  353.1 0.0 copy-start.7
  353.1 0.0 copy-start.6
  353.1 0.0 copy-start.5
  353.1 0.0 copy-start.4
  353.2 0.0 copy-start.3
  353.2 0.0 copy-start.2
  353.2 1.3 copy.43
  354.5 0.0 copy-done.7
  354.5 0.0 copy-start.1
  354.5 0.7 copy.44
  355.2 0.0 copy-done.6
  355.2 0.7 copy.45
  355.8 0.0 copy-done.5
  355.8 0.7 copy.46
  356.5 0.0 copy-done.4
  356.5 0.7 copy.47
  357.1 0.0 copy-done.3
  357.1 0.7 copy.48
  357.9 0.0 copy-done.2
  357.9 0.7 copy.49
  358.6 0.0 copy-done.1
  358.6 0.7 copy.50
  (2 shorter events, 0.0 us)
Async XLA Ops:
  347.1 4.2 %copy-start.8 = (f32[2,48,128]{2,1,0:T(8,128)S(1)}, f32[2,48,128]{2,1,0:T(8,128)}, u32[]{:S(2)}) copy-start(f32[2,48,128]{2,1,0:T(8,128)} %get-tuple-element.55) | copy-start | bytes 147460
  347.1 6.1 %copy-start = (bf16[2,512,1024]{2,1,0:T(8,128)(2,1)S(1)}, bf16[2,512,1024]{2,1,0:T(8,128)(2,1)}, u32[]{:S(2)}) copy-start(bf16[2,512,1024]{2,1,0:T(8,128)(2,1)} %get-tuple-element.94) | copy-start | bytes 6291460
  353.1 1.4 copy-start.7
  353.1 2.0 copy-start.6
  353.1 2.7 copy-start.5
  353.1 3.3 copy-start.4
  353.2 4.0 %copy-start.3 = (f32[64,1408]{1,0:T(8,128)S(1)}, f32[64,1408]{1,0:T(8,128)}, u32[]{:S(2)}) copy-start(f32[64,1408]{1,0:T(8,128)} %get-tuple-element.100) | copy-start | bytes 1081348
  353.2 4.7 %copy-start.2 = (f32[64,1408]{1,0:T(8,128)S(1)}, f32[64,1408]{1,0:T(8,128)}, u32[]{:S(2)}) copy-start(f32[64,1408]{1,0:T(8,128)} %get-tuple-element.101) | copy-start | bytes 1081348
  354.5 4.1 %copy-start.1 = (f32[64,1408]{1,0:T(8,128)S(1)}, f32[64,1408]{1,0:T(8,128)}, u32[]{:S(2)}) copy-start(f32[64,1408]{1,0:T(8,128)} %get-tuple-element.102) | copy-start | bytes 1081348

commit v2 on v1

--- a/solution.py
+++ b/solution.py
@@ -203,15 +203,18 @@
 
 
 def front_kernel(
-    shard_size, pieces, window, sizes,
+    shard_size, pieces, window, sizes, given,
     lengths_ref, gains_ref, query_ref, key_ref, value_ref, project_ref, gate_ref, up_ref, down_ref,
     inputs_ref, cots_ref, buckets_ref, table_ref,
     full_ref, normed_out, qkv_out, bandt_out, biast_out, grads_out, attended_out, tokens_own_ref,
-    lse_ref, output_ref, middle_grad_ref, gain_ref,
+    lse_ref, output_ref, middle_grad_ref, gain_ref, *rest,
+):
+    came_outs, rest = rest[: len(given)], rest[len(given) :]
+    (
     own_ref, tok, cot, band_raw, band, bandt, bias, biast, kaux, gain_buf, qkv, normed, scores, attended, project_w,
     normal, away, arrived, two_t, low_t, acc_out, acc_two, w_buf, g_buf, hid, ggate, gup,
-    send_sem, recv_sem, near_send, near_recv, local_sem, w_sem, g_sem, own_sem, bt_sem,
-):
+    send_sem, recv_sem, near_send, near_recv, local_sem, w_sem, g_sem, own_sem, bt_sem, early_send, early_recv,
+    ) = rest
     inner, hidden = sizes
     length, width = tok.shape
     half, quarter = length // 2, length // 4
@@ -527,6 +530,11 @@
             g_sem.at[j % 2],
         )
 
+    early_sums = []
+    for k, (a, b, name) in enumerate(given):
+        source = grads_out.at[:, :, 1 - x, :, a:b] if name == "x" else grads_out.at[:, 1 - place.y, :, :, a:b]
+        device = to_x if name == "x" else place.device(y=1 - place.y)
+        early_sums.append(send(source, came_outs[k], early_send.at[k], early_recv.at[k], device))
     gather.need(range(first_hidden_piece, first_hidden_piece + per_step))
     load_step(0).start()
     for j, units_here in enumerate(steps):
@@ -537,7 +545,11 @@
         def weight(k, slot=slot, n=n):
             return w_buf[slot, :, :, :, :, k * n : (k + 1) * n].reshape(width, n)
 
-        def rows_step(i, carry, j=j, n=n, weight=weight):
+        inside = gather.take(ROW_ACTS)
+
+        def rows_step(i, carry, j=j, n=n, weight=weight, inside=inside):
+            for k, act in enumerate(inside):
+                pl.when(i == (2 * k + 1) * (length // 256) // (2 * len(inside)))(act)
             rows = pl.ds(pl.multiple_of(i * 256, 256), 256)
             left, grad = two[rows, :], cot[rows, :]
             gate = jnp.dot(left, weight(0), preferred_element_type=jnp.float32)
@@ -559,11 +571,13 @@
             return carry
 
         lax.fori_loop(0, length // 256, rows_step, 0)
-        gather.run(1)
         if j + 1 < len(steps):
             first = first_hidden_piece + per_step * (j + 1)
             gather.need(range(first, first + per_step))
             load_step(j + 1).start()
+            if j + 2 == len(steps):
+                for copy in early_sums:
+                    copy.start()
         if j > 1:
             store_step(j - 2).wait()
 
@@ -637,12 +651,12 @@
     lax.fori_loop(0, length // 256, attended_step, 0)
     attended_store = own_load(10, attended, attended_out)
     attended_store.start()
-    for copy in (bandt_store, qkv_store, attended_store, project_store, *tokens_store):
+    for copy in (bandt_store, qkv_store, attended_store, project_store, *tokens_store, *early_sums):
         copy.wait()
     gather.sent()
 
 
-def front(shard_size, pieces, window, lengths, gains, weights, inputs, cots, buckets, table_rows):
+def front(shard_size, pieces, window, given, lengths, gains, weights, inputs, cots, buckets, table_rows):
     low, f32 = jnp.bfloat16, jnp.float32
     deep = shard_size // 2
     rows, inner = weights[0].shape
@@ -671,7 +685,7 @@
         shape((2, quarter, width), low),
         shape((2, quarter, width), f32),
         shape((2, 8, width), f32),
-    ]
+    ] + [shape((deep, 2, rows, b - a), low) for a, b, _ in given]
     scratch = [
         pltpu.VMEM((rows, wide), low),
         pltpu.VMEM((length, width), low),
@@ -709,12 +723,14 @@
         dma((2,)),
         dma((5 + 3 * len(hidden_steps(hidden)),)),
         dma((2,)),
+        dma((len(given),)),
+        dma((len(given),)),
     ]
     return pl.pallas_call(
-        functools.partial(front_kernel, shard_size, pieces, window, (inner, hidden)),
+        functools.partial(front_kernel, shard_size, pieces, window, (inner, hidden), given),
         out_shape=out_shape,
         in_specs=[pl.BlockSpec(memory_space=pltpu.SMEM)] + [hbm] * 11 + [vmem],
-        out_specs=[hbm] * 8 + [vmem] * 4,
+        out_specs=[hbm] * 8 + [vmem] * 4 + [hbm] * len(given),
         scratch_shapes=scratch,
         compiler_params=pltpu.CompilerParams(
             collective_id=1, has_side_effects=True, vmem_limit_bytes=60 * MIB
@@ -728,7 +744,8 @@
 
 
 class Scatter:
-    def __init__(self, place, pieces, sources, outs, buffers, sems):
+    def __init__(self, place, pieces, sources, outs, buffers, sems, came):
+        self.came = came
         self.place, self.pieces, self.sources, self.outs = place, pieces, sources, outs
         self.first, self.own, self.second, self.third = buffers
         self.own_sem, self.send_sem, self.recv_sem = sems
@@ -793,16 +810,25 @@
         for copy in self.copies(piece, hop):
             copy.wait_recv()
 
+    def came_copy(self, piece):
+        return pltpu.make_async_copy(self.came[piece], self.first[piece], self.recv_sem.at[piece, 0, 0])
+
     def begin(self, piece):
-        self.start(piece, 0)
+        if piece < len(self.came):
+            self.came_copy(piece).start()
+        else:
+            self.start(piece, 0)
         self.own_copy(piece).start()
 
     def add_first(self, piece):
         order = self.pieces[piece][3]
-        self.arrive(piece, 0)
+        if piece < len(self.came):
+            self.came_copy(piece).wait()
+        else:
+            self.arrive(piece, 0)
         self.own_copy(piece).wait()
-        if piece + self.window < self.early:
-            self.begin(piece + self.window)
+        if piece >= len(self.came) and self.waiting:
+            self.begin(self.waiting.pop(0))
         own, came = self.own[piece], self.first[piece]
         inner = own.shape[1]
 
@@ -856,8 +882,8 @@
         for out, start, at, n in self.pieces[piece][4]:
             self.outs[out][:, start : start + n] = total[:, at : at + n]
 
-    def plan(self, window, early):
-        self.window, self.early = window, early
+    def plan(self, window):
+        self.waiting = [i for i, piece in enumerate(self.pieces) if piece[0] == 0]
         count = len(self.pieces)
         for i in range(count + SUM_LAGS[1]):
             if i < count:
@@ -866,8 +892,8 @@
                 self.queue.append(functools.partial(self.add_second, i - SUM_LAGS[0]))
             if 0 <= i - SUM_LAGS[1] < count:
                 self.queue.append(functools.partial(self.add_third, i - SUM_LAGS[1]))
-        for i in range(min(window, early)):
-            self.begin(i)
+        for _ in range(min(len(self.came) + window, len(self.waiting))):
+            self.begin(self.waiting.pop(0))
 
     def run(self, steps):
         for _ in range(min(steps, len(self.queue))):
@@ -879,7 +905,7 @@
 
     def sent(self):
         for piece in range(len(self.pieces)):
-            for hop in range(3):
+            for hop in range(0 if piece >= len(self.came) else 1, 3):
                 for copy in self.copies(piece, hop):
                     copy.wait_send()
 
@@ -898,14 +924,14 @@
     return [tuple(shape) for shape in (first, left + tail, second, third)]
 
 
-def back_kernel(shard_size, pieces, early, sizes, *refs):
+def back_kernel(shard_size, pieces, sizes, given, *refs):
     inner, hidden, buckets = sizes
     count = len(pieces)
     (
         lengths_ref, full_ref, normed_in, qkv_in, bandt_in, biast_in, grads_in, do_in,
         lse_ref, output_ref, middle_ref, tokens_ref, gain_two_ref, table_ref,
     ) = refs[:14]
-    refs = refs[14:]
+    came, refs = refs[14 : 14 + given], refs[14 + given :]
     weight_outs, (output_out, input_out, small_out) = refs[:7], refs[7:10]
     refs = refs[10:]
     first, own, second, third = [refs[k * count : (k + 1) * count] for k in range(4)]
@@ -939,9 +965,9 @@
         copy.start()
     meet(place)
     scatter = Scatter(
-        place, pieces, (grads_in, wgrad), weight_outs, (first, own, second, third), (own_sem, send_sem, recv_sem),
+        place, pieces, (grads_in, wgrad), weight_outs, (first, own, second, third), (own_sem, send_sem, recv_sem), came,
     )
-    scatter.plan(SUM_WINDOW, early)
+    scatter.plan(SUM_WINDOW)
 
     def near(i, source, target, device):
         return send(source, target, near_send.at[i], near_recv.at[i], device)
@@ -1045,10 +1071,11 @@
 
             lax.fori_loop(0, width // 256, weight_step, 0)
 
-        for late in range(early, count):
-            @pl.when(unit == (late - early + 1) * per_pair - 1)
-            def _(late=late):
-                scatter.begin(late)
+        for late, piece in enumerate(pieces):
+            if piece[0]:
+                @pl.when(unit == piece[0] * per_pair - 1)
+                def _(late=late):
+                    scatter.begin(late)
 
         return carry
 
@@ -1182,7 +1209,7 @@
     scatter.sent()
 
 
-def back(shard_size, pieces, early, buckets, lengths, full, normed_t, qkv, bandt, biast, grads, do, lse, output, middle, tokens, gain_two, table_rows):
+def back(shard_size, pieces, buckets, lengths, full, normed_t, qkv, bandt, biast, grads, do, lse, output, middle, tokens, gain_two, table_rows, came):
     low, f32 = jnp.bfloat16, jnp.float32
     deep = shard_size // 2
     rows = full.shape[3]
@@ -1231,27 +1258,54 @@
         dma((9,)),
     ]
     return pl.pallas_call(
-        functools.partial(back_kernel, shard_size, pieces, early, (inner, hidden, buckets)),
+        functools.partial(back_kernel, shard_size, pieces, (inner, hidden, buckets), len(came)),
         out_shape=[
             *[shape((rows, n), f32) for n in (inner,) * 4 + (hidden,) * 3],
             shape((2, half, width), low),
             shape((2, half, width), low),
             shape((2, lines, 128), f32),
         ],
-        in_specs=[pl.BlockSpec(memory_space=pltpu.SMEM)] + [hbm] * 7 + [vmem] * 6,
+        in_specs=[pl.BlockSpec(memory_space=pltpu.SMEM)] + [hbm] * 7 + [vmem] * 6 + [hbm] * len(came),
         out_specs=[vmem] * 7 + [hbm, hbm, vmem],
         scratch_shapes=scratch,
         compiler_params=pltpu.CompilerParams(
             collective_id=2, has_side_effects=True, vmem_limit_bytes=60 * MIB
         ),
         name="back",
-    )(lengths, full, normed_t, qkv, bandt, biast, grads, do, lse, output, middle, tokens, gain_two, table_rows)
+    )(lengths, full, normed_t, qkv, bandt, biast, grads, do, lse, output, middle, tokens, gain_two, table_rows, *came)
+
+
+def finish_kernel(*refs):
+    count = len(refs) // 2
+    for source, target in zip(refs[:count], refs[count:]):
+        target[...] = source[...].astype(target.dtype)
+
+
+def finish(weight_sums, output, input_grad):
+    steps = 4 if weight_sums[0].shape[0] % 32 == 0 else 2
+    values = [*weight_sums, output, input_grad]
+    kinds = [jnp.float32] * len(weight_sums) + [output.dtype, jnp.float32]
+    specs = [pl.BlockSpec((w.shape[0] // steps, w.shape[1]), lambda i: (i, 0)) for w in weight_sums]
+    specs += [pl.BlockSpec((2, v.shape[1] // steps, v.shape[2]), lambda i: (0, i, 0)) for v in (output, input_grad)]
+    return pl.pallas_call(
+        finish_kernel,
+        grid=(steps,),
+        in_specs=specs,
+        out_specs=specs,
+        out_shape=[jax.ShapeDtypeStruct(v.shape, kind) for v, kind in zip(values, kinds)],
+        compiler_params=pltpu.CompilerParams(vmem_limit_bytes=60 * MIB),
+        name="finish",
+    )(*values)
 
 
 ORDERS = ("xyz", "zxy", "zyx", "zxy", "zxy", "zyx", "zxy", "zyx", "zxy")
-SUM_ORDERS = ("yxz", "xyz", "yzx", "yxz", "xzy", "yxz")
+SUM_ORDERS = ("yxz", "xyz", "yzx", "xzy", "yxz", "yxz")
+GIVEN = 4
+LATE_FIRST = 6
+LATE_STEP = 3
+ROW_ACTS = 2
 WINDOW = 4
-AHEAD = 4
+AHEAD = 2
 LAG = 3
 QUICK = 4
 SUM_WINDOW = 3
@@ -1291,10 +1345,10 @@
             if low < high:
                 segments.append((out, column + low - start, low - a, high - low))
         pieces.append((0, a, b, segments))
-    early = len(pieces)
     for pair in range(inner // 128):
-        pieces.append((1 + pair, 0, 3 * 128, [(t, pair * 128, t * 128, 128) for t in range(3)]))
-    return [(t, a, b, SUM_ORDERS[i % len(SUM_ORDERS)], segments) for i, (t, a, b, segments) in enumerate(pieces)], early
+        piece = (1 + pair, 0, 3 * 128, [(t, pair * 128, t * 128, 128) for t in range(3)])
+        pieces.insert(min(len(pieces), LATE_FIRST + LATE_STEP * pair), piece)
+    return [(t, a, b, SUM_ORDERS[i % len(SUM_ORDERS)], segments) for i, (t, a, b, segments) in enumerate(pieces)]
 
 
 def shards(
@@ -1308,6 +1362,7 @@
     bucket_count, heads = bias_table.shape
     rows, inner = query_weight.shape
     hidden = gate_weight.shape[1]
+    cuts = back_pieces(inner, hidden)
     gains = jnp.pad(jnp.stack([attention_gain, feedforward_gain], axis=1), ((0, 0), (0, 126)))
     table_rows = jnp.broadcast_to(
         jnp.pad(bias_table.astype(jnp.float32).T, ((0, 0), (0, 128 - bucket_count)))[:, None, :], (heads, 8, 128)
@@ -1315,16 +1370,16 @@
     weights = (query_weight, key_weight, value_weight, projection_weight, gate_weight, up_weight, down_weight)
     (
         full, normed_t, qkv, bandt, biast, grads, grad_attended, tokens,
-        lse, output, grad_middle, gain_two,
-    ) = front(shard_size, front_pieces(inner, hidden), WINDOW, lengths, gains, weights, inputs, cotangent, buckets, table_rows)
-
-    cuts, early = back_pieces(inner, hidden)
+        lse, output, grad_middle, gain_two, *came,
+    ) = front(shard_size, front_pieces(inner, hidden), WINDOW, [(a, b, order[0]) for _, a, b, order, _ in cuts[:GIVEN]], lengths, gains, weights, inputs, cotangent, buckets, table_rows)
+
     gain_two = jnp.sum(gain_two, axis=(0, 1)).reshape(-1, 128)
     *weight_sums, output, input_grad, small = back(
-        shard_size, cuts, early, bucket_count,
+        shard_size, cuts, bucket_count,
         lengths, full, normed_t, qkv, bandt, biast, grads, grad_attended,
-        lse, output, grad_middle, tokens, gain_two, table_rows,
+        lse, output, grad_middle, tokens, gain_two, table_rows, came,
     )
+    *weight_sums, output, input_grad = finish(weight_sums, output, input_grad)
     lines = width // 128
     me = lax.axis_index("shard") * 2 + x
 
@@ -1332,7 +1387,7 @@
         return lax.dynamic_slice_in_dim(small[1, part * lines : (part + 1) * lines].reshape(-1), me * rows, rows)
 
     return (
-        output, input_grad.astype(jnp.float32),
+        output, input_grad,
         *weight_sums, own_gain(0), own_gain(1), small[0, 2 * lines :, :heads],
     )
 

time: 360 us -> 351 us (0.975)
  local copies, waits for them, and re-layouts: 10.7 us -> 4.49 us
  other arithmetic: 7.03 us -> 2.81 us
    pallas_call x1 -> x2, Pallas kernels: 163 us -> 171 us  [the longest x1 164 us: back(): pl.pallas_call(functools.partial(back_kernel, shard_size, pieces, (inner,...]
    pallas_call x1, Pallas kernels: 178 us -> 172 us  [front(): pl.pallas_call(functools.partial(front_kernel, shard_size, pieces, window...]
    unnamed x28 -> x4, local copies, waits for them, and re-layouts: 8.14 us -> 1.96 us
    convert_element_type x1 -> x0, other arithmetic: 4.22 us -> none  [shards(): input_grad.astype(jnp.float32)]
where the time goes in v2:
time: 351 us; the launch traced here: 350 us
  Pallas kernels  342 us (97%)
  local copies, waits for them, and re-layouts  4.49 us (1%)
    pallas_call x1, Pallas kernels, front(): pl.pallas_call(functools.partial(front_kernel, shard_size, pieces, window...  172 us
    pallas_call x1, Pallas kernels, back(): pl.pallas_call(functools.partial(back_kernel, shard_size, pieces, (inner,...  164 us

profile of v2, /device:TPU:0, one launch (start us, length us, event | category | flops | bytes accessed | tf_op | source)
XLA Modules:
  0.0 350.1 jit_solution(6069214991368741074)
XLA Ops:
  0.6 0.7 pad_convert_fusion
  1.3 0.6 broadcast_in_dim.2.table_ref.refs_13_
  1.9 1.3 copy.33.lengths_ref.refs_0_
  3.2 0.7 pad_maximum_fusion
  3.9 0.1 copy.31
  4.0 0.6 pad.11.gains_ref
  4.7 171.5 %front.1 = (bf16[4,2,2,64,6400]{4,3,2,1,0:T(8,128)(2,1)}, bf16[1024,1024]{1,0:T(8,128)(2,1)}, bf16[12,1024,128]{2,1,0:T(8,128)(2,1)}, bf16[8,384,128]{2,1,0:T(8,...) custom-call(s32[2,1]{1,0:T(2,128)} %copy.33.lengths_ref.refs_0_, ...), custom_call_target="tpu_custom_call" | custom-call | tf_op jit(solution)/shard_map/front/pallas_call | solution.py:729
  176.2 1.4 reduce_sum.9
  177.6 164.4 %back.1 = (f32[64,512]{1,0:T(8,128)}, f32[64,512]{1,0:T(8,128)}, f32[64,512]{1,0:T(8,128)}, f32[64,512]{1,0:T(8,128)}, f32[64,1408]{1,0:T(8,128)}, /*index=5*/f3...) custom-call(s32[2,1]{1,0:T(2,128)} %copy.33.lengths_ref.refs_0_, ...), custom_call_target="tpu_custom_call" | custom-call | tf_op jit(solution)/shard_map/back/pallas_call | solution.py:1260
  342.0 0.0 copy-start
  342.0 6.2 %finish.1 = (f32[64,512]{1,0:T(8,128)}, f32[64,512]{1,0:T(8,128)}, f32[64,512]{1,0:T(8,128)}, f32[64,512]{1,0:T(8,128)}, f32[64,1408]{1,0:T(8,128)}, /*index=5*/...) custom-call(f32[64,512]{1,0:T(8,128)} %get-tuple-element.63.refs_0_, ...), custom_call_target="tpu_custom_call" | custom-call | tf_op jit(solution)/shard_map/finish/pallas_call | solution.py:1290
  348.2 0.0 copy-done
  348.2 0.6 dynamic_slice.6
  348.8 0.6 dynamic_slice.7
  349.4 0.7 copy.34
  (2 shorter events, 0.0 us)
Async XLA Ops:
  342.0 6.2 %copy-start = (f32[2,48,128]{2,1,0:T(8,128)S(1)}, f32[2,48,128]{2,1,0:T(8,128)}, u32[]{:S(2)}) copy-start(f32[2,48,128]{2,1,0:T(8,128)} %get-tuple-element.81) | copy-start | bytes 147460

commit v3 on v2

--- a/solution.py
+++ b/solution.py
@@ -575,11 +575,13 @@
             first = first_hidden_piece + per_step * (j + 1)
             gather.need(range(first, first + per_step))
             load_step(j + 1).start()
-            if j + 2 == len(steps):
-                for copy in early_sums:
-                    copy.start()
         if j > 1:
             store_step(j - 2).wait()
+        if j + 2 >= len(steps):
+            for copy, (_, b, _) in zip(early_sums, given):
+                ready = max(0, -(-b // (3 * HIDDEN_STEP)) - 1)
+                if ready == j - 2 or (ready < j - 2 and j + 2 == len(steps)):
+                    copy.start()
 
         tiles = width // 256
 
@@ -1170,7 +1172,9 @@
     lines = width // 128
     for i in range(lines):
         small[i : i + 1, :] = gain_sum[:, i * 128 : (i + 1) * 128]
-    small[lines : 2 * lines, :] = gain_two_ref[...]
+    gain_two_sum = jnp.sum(gain_two_ref[0] + gain_two_ref[1], axis=0, keepdims=True)
+    for i in range(lines):
+        small[lines + i : lines + i + 1, :] = gain_two_sum[:, i * 128 : (i + 1) * 128]
     small[2 * lines : 2 * lines + buckets, :] = table
     small_base = 10
 
@@ -1299,8 +1303,8 @@
 
 
 ORDERS = ("xyz", "zxy", "zyx", "zxy", "zxy", "zyx", "zxy", "zyx", "zxy")
-SUM_ORDERS = ("yxz", "xyz", "yzx", "xzy", "yxz", "yxz")
-GIVEN = 4
+SUM_ORDERS = ("yxz", "xyz")
+GIVEN = 6
 LATE_FIRST = 6
 LATE_STEP = 3
 ROW_ACTS = 2
@@ -1311,9 +1315,9 @@
 SUM_WINDOW = 3
 SUM_LAGS = (2, 4)
 FORWARD_ACTS = 8
-ATTENTION_ACTS = 20
-ACT_FIRST = 5
-TABLE_ACTS = 7
+ATTENTION_ACTS = 28
+ACT_FIRST = 2
+TABLE_ACTS = 14
 
 
 def front_pieces(inner, hidden):
@@ -1373,7 +1377,6 @@
         lse, output, grad_middle, gain_two, *came,
     ) = front(shard_size, front_pieces(inner, hidden), WINDOW, [(a, b, order[0]) for _, a, b, order, _ in cuts[:GIVEN]], lengths, gains, weights, inputs, cotangent, buckets, table_rows)
 
-    gain_two = jnp.sum(gain_two, axis=(0, 1)).reshape(-1, 128)
     *weight_sums, output, input_grad, small = back(
         shard_size, cuts, bucket_count,
         lengths, full, normed_t, qkv, bandt, biast, grads, grad_attended,

time: 351 us -> 336 us (0.957)
  Pallas kernels: 342 us -> 329 us
    pallas_call x1, Pallas kernels: 164 us -> 145 us  [back(): pl.pallas_call(functools.partial(back_kernel, shard_size, pieces, (inner,...]
    pallas_call x1, Pallas kernels: 172 us -> 177 us  [front(): pl.pallas_call(functools.partial(front_kernel, shard_size, pieces, window...]
where the time goes in v3:
time: 336 us; the launch traced here: 335 us
  Pallas kernels  329 us (98%)
  local copies, waits for them, and re-layouts  4.49 us (1%)
    pallas_call x1, Pallas kernels, front(): pl.pallas_call(functools.partial(front_kernel, shard_size, pieces, window...  177 us
    pallas_call x1, Pallas kernels, back(): pl.pallas_call(functools.partial(back_kernel, shard_size, pieces, (inner,...  145 us

profile of v3, /device:TPU:0, one launch (start us, length us, event | category | flops | bytes accessed | tf_op | source)
XLA Modules:
  0.0 335.5 jit_solution(7305568411567457642)
XLA Ops:
  0.6 0.7 pad_convert_fusion
  1.3 0.6 broadcast_in_dim.2.table_ref.refs_13_
  1.9 1.3 copy.33.lengths_ref.refs_0_
  3.2 0.7 pad_maximum_fusion
  3.9 0.1 copy.31
  4.0 0.6 pad.11.gains_ref
  4.7 177.3 %front.1 = (bf16[4,2,2,64,6400]{4,3,2,1,0:T(8,128)(2,1)}, bf16[1024,1024]{1,0:T(8,128)(2,1)}, bf16[12,1024,128]{2,1,0:T(8,128)(2,1)}, bf16[8,384,128]{2,1,0:T(8,...) custom-call(s32[2,1]{1,0:T(2,128)} %copy.33.lengths_ref.refs_0_, ...), custom_call_target="tpu_custom_call" | custom-call | tf_op jit(solution)/shard_map/front/pallas_call | solution.py:731
  182.0 145.5 %back.1 = (f32[64,512]{1,0:T(8,128)}, f32[64,512]{1,0:T(8,128)}, f32[64,512]{1,0:T(8,128)}, f32[64,512]{1,0:T(8,128)}, f32[64,1408]{1,0:T(8,128)}, /*index=5*/f3...) custom-call(s32[2,1]{1,0:T(2,128)} %copy.33.lengths_ref.refs_0_, ...), custom_call_target="tpu_custom_call" | custom-call | tf_op jit(solution)/shard_map/back/pallas_call | solution.py:1264
  327.4 0.0 copy-start
  327.4 6.2 %finish.1 = (f32[64,512]{1,0:T(8,128)}, f32[64,512]{1,0:T(8,128)}, f32[64,512]{1,0:T(8,128)}, f32[64,512]{1,0:T(8,128)}, f32[64,1408]{1,0:T(8,128)}, /*index=5*/...) custom-call(f32[64,512]{1,0:T(8,128)} %get-tuple-element.67.refs_0_, ...), custom_call_target="tpu_custom_call" | custom-call | tf_op jit(solution)/shard_map/finish/pallas_call | solution.py:1294
  333.6 0.0 copy-done
  333.6 0.6 dynamic_slice.6
  334.2 0.6 dynamic_slice.7
  334.8 0.7 copy.34
  (2 shorter events, 0.0 us)
Async XLA Ops:
  327.4 6.2 %copy-start = (f32[2,48,128]{2,1,0:T(8,128)S(1)}, f32[2,48,128]{2,1,0:T(8,128)}, u32[]{:S(2)}) copy-start(f32[2,48,128]{2,1,0:T(8,128)} %get-tuple-element.85) | copy-start | bytes 147460

commit v4 on v3

--- a/solution.py
+++ b/solution.py
@@ -1310,11 +1310,11 @@
 ROW_ACTS = 2
 WINDOW = 4
 AHEAD = 2
-LAG = 3
+LAG = 4
 QUICK = 4
 SUM_WINDOW = 3
 SUM_LAGS = (2, 4)
-FORWARD_ACTS = 8
+FORWARD_ACTS = 9
 ATTENTION_ACTS = 28
 ACT_FIRST = 2
 TABLE_ACTS = 14

time: 336 us -> 334 us (level)
  no operation moved by 1% of the time
where the time goes in v4:
time: 334 us; the launch traced here: 333 us
  Pallas kernels  327 us (98%)
  local copies, waits for them, and re-layouts  4.49 us (1%)
    pallas_call x1, Pallas kernels, front(): pl.pallas_call(functools.partial(front_kernel, shard_size, pieces, window...  176 us
    pallas_call x1, Pallas kernels, back(): pl.pallas_call(functools.partial(back_kernel, shard_size, pieces, (inner,...  144 us

profile of v4, /device:TPU:0, one launch (start us, length us, event | category | flops | bytes accessed | tf_op | source)
XLA Modules:
  0.0 333.4 jit_solution(4393522416069732903)
XLA Ops:
  0.6 0.7 pad_convert_fusion
  1.3 0.6 broadcast_in_dim.2.table_ref.refs_13_
  1.9 1.3 copy.33.lengths_ref.refs_0_
  3.2 0.7 pad_maximum_fusion
  3.9 0.1 copy.31
  4.0 0.6 pad.11.gains_ref
  4.7 176.2 %front.1 = (bf16[4,2,2,64,6400]{4,3,2,1,0:T(8,128)(2,1)}, bf16[1024,1024]{1,0:T(8,128)(2,1)}, bf16[12,1024,128]{2,1,0:T(8,128)(2,1)}, bf16[8,384,128]{2,1,0:T(8,...) custom-call(s32[2,1]{1,0:T(2,128)} %copy.33.lengths_ref.refs_0_, ...), custom_call_target="tpu_custom_call" | custom-call | tf_op jit(solution)/shard_map/front/pallas_call | solution.py:731
  180.9 144.5 %back.1 = (f32[64,512]{1,0:T(8,128)}, f32[64,512]{1,0:T(8,128)}, f32[64,512]{1,0:T(8,128)}, f32[64,512]{1,0:T(8,128)}, f32[64,1408]{1,0:T(8,128)}, /*index=5*/f3...) custom-call(s32[2,1]{1,0:T(2,128)} %copy.33.lengths_ref.refs_0_, ...), custom_call_target="tpu_custom_call" | custom-call | tf_op jit(solution)/shard_map/back/pallas_call | solution.py:1264
  325.4 0.0 copy-start
  325.4 6.2 %finish.1 = (f32[64,512]{1,0:T(8,128)}, f32[64,512]{1,0:T(8,128)}, f32[64,512]{1,0:T(8,128)}, f32[64,512]{1,0:T(8,128)}, f32[64,1408]{1,0:T(8,128)}, /*index=5*/...) custom-call(f32[64,512]{1,0:T(8,128)} %get-tuple-element.67.refs_0_, ...), custom_call_target="tpu_custom_call" | custom-call | tf_op jit(solution)/shard_map/finish/pallas_call | solution.py:1294
  331.5 0.0 copy-done
  331.6 0.6 dynamic_slice.6
  332.2 0.6 dynamic_slice.7
  332.8 0.7 copy.34
  (2 shorter events, 0.0 us)
Async XLA Ops:
  325.4 6.2 %copy-start = (f32[2,48,128]{2,1,0:T(8,128)S(1)}, f32[2,48,128]{2,1,0:T(8,128)}, u32[]{:S(2)}) copy-start(f32[2,48,128]{2,1,0:T(8,128)} %get-tuple-element.85) | copy-start | bytes 147460

commit v5 on v4

--- a/solution.py
+++ b/solution.py
@@ -266,9 +266,8 @@
     for copy in (*own_loads, *own_bands, own_tok, own_cot):
         copy.start()
     meet(place)
-    for copy in own_loads:
+    for copy in own_loads[:4]:
         copy.wait()
-    own_full.start()
 
     gather = Gather(place, pieces, own_ref, full_ref, send_sem, recv_sem)
     to_x, to_c = place.device(x=1 - x), place.device(c=1 - c)
@@ -287,7 +286,10 @@
     band_c = [near(16 + len(mine) + i, band.at[block], band.at[block], to_c) for i, block in enumerate(theirs)]
     tok_c = near(4, tok.at[x_rows(1 - x, c)], tok.at[x_rows(1 - x, c)], to_c)
     cot_c = near(5, cot.at[x_rows(1 - x, c)], cot.at[x_rows(1 - x, c)], to_c)
-    gather.plan(window)
+    gather.plan(min(window, len(qkv_pieces)))
+    for copy in own_loads[4:]:
+        copy.wait()
+    own_full.start()
     for copy in own_bands:
         copy.wait()
     for i in range(blocks // 2):

time: 334 us -> 334 us (level)
  no operation moved by 1% of the time
where the time goes in v5:
time: 334 us; the launch traced here: 333 us
  Pallas kernels  327 us (98%)
  local copies, waits for them, and re-layouts  4.49 us (1%)
    pallas_call x1, Pallas kernels, front(): pl.pallas_call(functools.partial(front_kernel, shard_size, pieces, window...  176 us
    pallas_call x1, Pallas kernels, back(): pl.pallas_call(functools.partial(back_kernel, shard_size, pieces, (inner,...  145 us

profile of v5, /device:TPU:0, one launch (start us, length us, event | category | flops | bytes accessed | tf_op | source)
XLA Modules:
  0.0 333.5 jit_solution(13042967288848034369)
XLA Ops:
  0.6 0.7 pad_convert_fusion
  1.3 0.6 broadcast_in_dim.2.table_ref.refs_13_
  1.9 1.3 copy.33.lengths_ref.refs_0_
  3.2 0.7 pad_maximum_fusion
  3.9 0.1 copy.31
  4.0 0.6 pad.11.gains_ref
  4.7 175.9 %front.1 = (bf16[4,2,2,64,6400]{4,3,2,1,0:T(8,128)(2,1)}, bf16[1024,1024]{1,0:T(8,128)(2,1)}, bf16[12,1024,128]{2,1,0:T(8,128)(2,1)}, bf16[8,384,128]{2,1,0:T(8,...) custom-call(s32[2,1]{1,0:T(2,128)} %copy.33.lengths_ref.refs_0_, ...), custom_call_target="tpu_custom_call" | custom-call | tf_op jit(solution)/shard_map/front/pallas_call | solution.py:733
  180.5 144.9 %back.1 = (f32[64,512]{1,0:T(8,128)}, f32[64,512]{1,0:T(8,128)}, f32[64,512]{1,0:T(8,128)}, f32[64,512]{1,0:T(8,128)}, f32[64,1408]{1,0:T(8,128)}, /*index=5*/f3...) custom-call(s32[2,1]{1,0:T(2,128)} %copy.33.lengths_ref.refs_0_, ...), custom_call_target="tpu_custom_call" | custom-call | tf_op jit(solution)/shard_map/back/pallas_call | solution.py:1266
  325.5 0.0 copy-start
  325.5 6.2 %finish.1 = (f32[64,512]{1,0:T(8,128)}, f32[64,512]{1,0:T(8,128)}, f32[64,512]{1,0:T(8,128)}, f32[64,512]{1,0:T(8,128)}, f32[64,1408]{1,0:T(8,128)}, /*index=5*/...) custom-call(f32[64,512]{1,0:T(8,128)} %get-tuple-element.67.refs_0_, ...), custom_call_target="tpu_custom_call" | custom-call | tf_op jit(solution)/shard_map/finish/pallas_call | solution.py:1296
  331.6 0.0 copy-done
  331.7 0.6 dynamic_slice.6
  332.2 0.6 dynamic_slice.7
  332.8 0.7 copy.34
  (2 shorter events, 0.0 us)
Async XLA Ops:
  325.5 6.2 %copy-start = (f32[2,48,128]{2,1,0:T(8,128)S(1)}, f32[2,48,128]{2,1,0:T(8,128)}, u32[]{:S(2)}) copy-start(f32[2,48,128]{2,1,0:T(8,128)} %get-tuple-element.85) | copy-start | bytes 147460
